TPU v7x, 128 devices: a whole 4x4x4 slice. The times are simulated.
128 devices in a mesh: cluster: 8 (over z, core), member: 16 (over y, x).
Axes of the slice: x: 4, y: 4, z: 4, core: 2. Of those that a mesh axis runs over, the one named last changes fastest.
Arguments:
- cam_jac: bfloat16 [18, 8, 65536], P(None, None, ('cluster', 'member')), may hold values from -0.3125 to 0.3125
- point_jac: bfloat16 [6, 8, 65536], P(None, None, ('cluster', 'member')), may hold values from -6 to 6
- residuals: bfloat16 [2, 8, 65536], P(None, None, ('cluster', 'member')), may hold values from -6 to 6
- obs_camera: int32 [8, 65536], P(None, ('cluster', 'member')), may hold values from 0 to 2047, as said below
- obs_count: int32 [65536], P(('cluster', 'member')), may hold values from 2 to 8, as said below
- new_cluster: int32 [2048], replicated, may hold values from 0 to 7, as said below
- new_slot: int32 [2048], replicated, may hold values from 0 to 255, as said below
Outputs:
- reduced_system: float32 [18432, 2304], P(('cluster', 'member'))
- camera_step: float32 [18432], P(('cluster', 'member'))
Inputs may be any that keep to these rules, and one draw needn't show every extreme that they name: `obs_camera`: old ids: camera i lies in old cluster i // 256; a point block stored on the devices of cluster c observes cameras of old cluster c only, distinct ones in all its slots. Its live observations lie in new cluster c except at most two that lie in a single other new cluster. On every device, for each other cluster, at most 16 point blocks have live observations there, and exactly 16 for some other cluster. `obs_count`: some point block of every device has 8 live observations. `new_cluster`: each old cluster keeps all but 64 of its cameras; every new cluster holds exactly 256 cameras. `new_slot`: cameras of one new cluster have distinct rows.
All inputs are finite; a program needn't handle non-finite values.
Results may differ from a plain program's by a relative error of at most 0.0038.
Values may be sent and summed in bfloat16 or wider, within the bound.
No kernel may reach another device: no remote copies, remote signals or barrier semaphores. Data moves between devices by JAX's collectives and lax.ppermute only.
A program may use at most 192 MiB of HBM per device.

v0:
```python
import jax
import jax.numpy as jnp
from jax import lax
from jax.sharding import PartitionSpec as P

SHOTS_EACH_BATCH = 256
PANEL = 16
BCAP = 16


DAMPING = 0.5
EXACT_PRECISION = lax.Precision.HIGHEST


def invert_three(matrix):

    def cofactor(i, j):
        keep_rows = [r for r in range(3) if r != i]
        keep_cols = [r for r in range(3) if r != j]
        minor_value = (
            matrix[keep_rows[0], keep_cols[0]] * matrix[keep_rows[1], keep_cols[1]]
            - matrix[keep_rows[0], keep_cols[1]] * matrix[keep_rows[1], keep_cols[0]]
        )
        sign_value = 1.0 if (i + j) % 2 == 0 else -1.0
        return sign_value * minor_value

    cofactors = [[cofactor(i, j) for j in range(3)] for i in range(3)]
    determinant = (
        matrix[0, 0] * cofactors[0][0]
        + matrix[0, 1] * cofactors[0][1]
        + matrix[0, 2] * cofactors[0][2]
    )
    adjugate = jnp.stack([jnp.stack([cofactors[j][i] for j in range(3)]) for i in range(3)])
    return adjugate / determinant


def eliminate(cam_part, point_part, resid_part, slot_rows):
    valid_mask = (slot_rows >= 0).astype(jnp.float32)
    obs_slots = slot_rows.shape[0]
    block_count = slot_rows.shape[1]
    camera_rows = (cam_part.astype(jnp.float32) * valid_mask).reshape(2, 9, obs_slots, block_count)
    point_rows = (point_part.astype(jnp.float32) * valid_mask).reshape(2, 3, obs_slots, block_count)
    resid_rows = resid_part.astype(jnp.float32) * valid_mask
    normal_point = (
        jnp.einsum("kbon,kcon->bcn", point_rows, point_rows, precision=EXACT_PRECISION)
        + DAMPING * jnp.eye(3, dtype=jnp.float32)[:, :, None]
    )
    point_grad = jnp.einsum("kbon,kon->bn", point_rows, resid_rows, precision=EXACT_PRECISION)
    landmark_inverse_tiles = invert_three(normal_point)
    camera_point_coupling = jnp.einsum(
        "kaon,kbon->abon", camera_rows, point_rows, precision=EXACT_PRECISION
    ).astype(jnp.bfloat16)
    reduced_camera_matrix = jnp.einsum(
        "wrsd,rpd->wpsd",
        camera_point_coupling.astype(jnp.float32),
        landmark_inverse_tiles,
        precision=EXACT_PRECISION,
    ).astype(jnp.bfloat16)
    camera_normal = jnp.einsum(
        "kaon,kcon->acon", camera_rows, camera_rows, precision=EXACT_PRECISION
    )
    camera_grad = jnp.einsum(
        "kaon,kon->aon", camera_rows, resid_rows, precision=EXACT_PRECISION
    ) - jnp.einsum(
        "abon,bn->aon",
        reduced_camera_matrix.astype(jnp.float32),
        point_grad,
        precision=EXACT_PRECISION,
    )
    camera_terms = jnp.concatenate(
        [camera_normal.reshape(81, obs_slots, block_count), camera_grad], axis=0
    )
    return (camera_point_coupling, reduced_camera_matrix, camera_terms)


def collect_cameras(camera_terms, slot_rows):
    camera_ids = jnp.arange(SHOTS_EACH_BATCH, dtype=jnp.int32)
    total = jnp.zeros((90, SHOTS_EACH_BATCH), jnp.float32)
    for obs_index in range(slot_rows.shape[0]):
        onehot = (slot_rows[obs_index][:, None] == camera_ids[None, :]).astype(jnp.float32)
        total = total + jnp.dot(camera_terms[:, obs_index, :], onehot, precision=EXACT_PRECISION)
    return total


def place_blocks(values, slot_rows, first_camera, camera_count):
    block_count = slot_rows.shape[1]
    cameras = first_camera + jnp.arange(camera_count, dtype=jnp.int32)
    onehot = (slot_rows[None, :, :] == cameras[:, None, None]).astype(jnp.bfloat16)
    placed = jnp.einsum("iop,abop->iabp", onehot, values, preferred_element_type=jnp.bfloat16)
    return placed.reshape(camera_count * 9, 3 * block_count)


def schur_rows(camera_point_coupling, reduced_camera_matrix, slot_rows, first_camera, camera_count):
    left_side = place_blocks(reduced_camera_matrix, slot_rows, first_camera, camera_count)
    right_side = place_blocks(camera_point_coupling, slot_rows, 0, SHOTS_EACH_BATCH)
    return jnp.einsum("rk,ck->rc", left_side, right_side, preferred_element_type=jnp.float32)


def per_device(cam_jac, point_jac, residuals, obs_camera, obs_count, new_cluster, new_slot):
    cluster_count = lax.axis_size("cluster")
    member_count = lax.axis_size("member")
    my_cluster = lax.axis_index("cluster")
    my_member = lax.axis_index("member")
    live_mask = lax.broadcasted_iota(jnp.int32, obs_camera.shape, 0) < obs_count[None, :]
    cluster_of = jnp.take(new_cluster, obs_camera)
    row_of = jnp.take(new_slot, obs_camera)
    at_home = live_mask & (cluster_of == my_cluster)
    abroad = live_mask & (cluster_of != my_cluster)
    home_slots = jnp.where(at_home, row_of, -1)
    aimed_batch = jnp.max(jnp.where(abroad, cluster_of, -1), axis=0)
    target_hits = (
        aimed_batch[None, :] == jnp.arange(cluster_count, dtype=jnp.int32)[:, None]
    ).astype(jnp.int32)
    destination_rank = jnp.sum((jnp.cumsum(target_hits, axis=1) - 1) * target_hits, axis=0)
    column = jnp.where(aimed_batch >= 0, aimed_batch * BCAP + destination_rank, -1)
    chooser = (
        column[:, None] == jnp.arange(cluster_count * BCAP, dtype=jnp.int32)[None, :]
    ).astype(jnp.bfloat16)
    outgoing = abroad.astype(jnp.bfloat16)[None]
    slot_code = jnp.where(abroad, row_of + 1, 0).astype(jnp.bfloat16)[None]
    payload = jnp.concatenate(
        [cam_jac * outgoing, point_jac * outgoing, residuals * outgoing, slot_code], axis=0
    )
    packed_blocks = jnp.einsum(
        "kop,ps->kos", payload, chooser, preferred_element_type=jnp.float32
    ).astype(jnp.bfloat16)
    arrived = lax.all_to_all(packed_blocks, "cluster", split_axis=2, concat_axis=2, tiled=True)
    home_coupling, home_reduced, resident_summands = eliminate(
        cam_jac, point_jac, residuals, home_slots
    )
    far_slots = arrived[26].astype(jnp.int32) - 1
    far_coupling, far_reduced, far_terms = eliminate(
        arrived[:18], arrived[18:24], arrived[24:26], far_slots
    )
    camera_total = collect_cameras(resident_summands, home_slots) + collect_cameras(
        far_terms, far_slots
    )
    owned_sums = lax.psum_scatter(camera_total, "member", scatter_dimension=1, tiled=True)
    camera_point_coupling = jnp.concatenate([home_coupling, far_coupling], axis=3)
    reduced_camera_matrix = jnp.concatenate([home_reduced, far_reduced], axis=3)
    slot_rows = jnp.concatenate([home_slots, far_slots], axis=1)
    camera_share = SHOTS_EACH_BATCH // member_count
    row_count = 9 * camera_share
    first_camera = my_member * camera_share
    summed = lax.psum_scatter(
        schur_rows(
            camera_point_coupling,
            reduced_camera_matrix,
            slot_rows,
            jnp.int32(0) // 9,
            row_count * lax.axis_size("member") // 9,
        ),
        "member",
        scatter_dimension=0,
        tiled=True,
    )
    normal_blocks = (
        owned_sums[:81].reshape(9, 9, camera_share)
        + DAMPING * jnp.eye(9, dtype=jnp.float32)[:, :, None]
    )
    own_columns = (
        (first_camera + jnp.arange(camera_share, dtype=jnp.int32))[:, None]
        == jnp.arange(SHOTS_EACH_BATCH, dtype=jnp.int32)[None, :]
    ).astype(jnp.float32)
    block_diag = (
        normal_blocks.transpose(2, 0, 1)[:, :, None, :] * own_columns[:, None, :, None]
    ).reshape(row_count, 9 * SHOTS_EACH_BATCH)
    reduced_matrix = block_diag - summed
    gradient = owned_sums[81:].T.reshape(-1)
    panel_width = 9 * PANEL
    panel_count = camera_share // PANEL
    square = lax.dynamic_slice_in_dim(reduced_matrix, first_camera * 9, row_count, 1)
    diagonal = jnp.stack([square])
    factor = jnp.linalg.cholesky(diagonal)
    solved = jax.scipy.linalg.cho_solve(
        (factor, True), gradient.reshape(panel_count, panel_width)[..., None]
    )[..., 0]
    return (reduced_matrix, -solved.reshape(-1))


def solution(mesh):
    in_specs = (
        P(None, None, ("cluster", "member")),
        P(None, None, ("cluster", "member")),
        P(None, None, ("cluster", "member")),
        P(None, ("cluster", "member")),
        P(("cluster", "member")),
        P(),
        P(),
    )
    out_specs = (P(("cluster", "member"), None), P(("cluster", "member")))
    return jax.shard_map(
        per_device, mesh=mesh, in_specs=in_specs, out_specs=out_specs, check_vma=False
    )
```

profile of v0, /device:TPU:0, one launch (start us, length us, event | category | flops | bytes accessed | tf_op | source)
XLA Modules:
  0.0 706.5 jit_solution(15574909956249831799)
XLA Ops:
  7.9 23.0 %gather_fusion.1 = s32[4096]{0:T(1024)S(1)} fusion(s32[2048]{0:T(1024)S(1)} %copy-done, s32[4096]{0:T(1024)S(1)} %broadcast_clamp_fusion), kind=kCustom, calls=%fused_computation.1.clone | custom fusion | bytes 49152 | tf_op jit(solution)/shard_map/jit(_take)/gather | solution.py:106
  31.7 23.0 %gather_fusion = s32[4096]{0:T(1024)S(1)} fusion(s32[2048]{0:T(1024)S(1)} %copy-done.2, s32[4096]{0:T(1024)S(1)} %broadcast_clamp_fusion), kind=kCustom, calls=%fused_computation.clone | custom fusion | bytes 49152 | tf_op jit(solution)/shard_map/jit(_take)/gather | solution.py:105
  76.9 11.9 %multiply_subtract_fusion.1 = (f32[1,1,512]{0,1,2:T(1,128)S(1)}, f32[1,1,512]{0,1,2:T(1,128)S(1)}, f32[512]{0:T(512)S(1)}, f32[512]{0:T(512)S(1)}, f32[512]{0:T(512)S(1)}) fusion(f32[3,3,512]{0,1,2:T(4,128)S(1)} %fusion.14), kind=kLoop, calls=%fused_computation.117 | loop fusion | flops 8192 | bytes 28672 | tf_op jit(solution)/shard_map/sub | solution.py:21
  88.8 13.2 %add_reduce_fusion = (f32[512]{0:T(512)S(1)}, f32[512]{0:T(512)S(1)}, f32[512]{0:T(512)S(1)}, f32[512]{0:T(512)S(1)}, f32[512]{0:T(512)S(1)}, /*index=5*/f32[512]{0:T(512)S(1)}, f32[512]{0:T(512)S(1)}) fusion(f32[1,1,512]{0,1,2:T(1,128)S(1)} %get-tuple-element.57, f32[1,1,512]{0,1,2:T(1,128)S(1)} %get-tuple-element.56, f32[3,3,512]{0,1,2:T(4,128)S(1)} %fusion.14), kind=kLoop, calls=%fused_computation.108 | loop fusion | flops 10240 | bytes 34816 | tf_op jit(solution)/shard_map/add | solution.py:29
  105.6 57.6 %convolution_bitcast_fusion = f32[9,9,8,512]{0,1,3,2:T(8,128)} fusion(f32[2,9,8,512]{1,0,3,2:T(2,128)} %copy.189), kind=kOutput, calls=%fused_computation.2 | convolution fusion | flops 7962624 | bytes 1622016 | tf_op jit(solution)/shard_map/kaon,kcon->acon/dot_general | solution.py:59
  163.2 34.1 %fusion.9 = bf16[9,3,8,512]{0,1,3,2:T(4,128)(2,1)S(1)} fusion(f32[2,3,8,512]{1,0,3,2:T(2,128)S(1)} %copy-done.7, f32[2,9,8,512]{1,0,3,2:T(2,128)S(1)} %copy-done.3), kind=kOutput, calls=%fused_computation.23 | convolution fusion | flops 2764800 | bytes 614400 | tf_op jit(solution)/shard_map/kaon,kbon->abon/dot_general | solution.py:50
  214.9 15.8 %copy.191 = f32[9,9,8,512]{3,2,1,0:T(8,128)S(1)} copy(f32[9,9,8,512]{0,1,3,2:T(8,128)} %convolution_bitcast_fusion) | data formatting | bytes 2654208 | tf_op jit(solution)/shard_map/kaon,kcon->acon/transpose | solution.py:59
  250.7 16.0 %convolution_bitcast_fusion.3 = f32[9,9,8,128]{0,1,3,2:T(8,128)} fusion(f32[2,9,8,128]{1,0,3,2:T(2,128)S(1)} %copy.201), kind=kOutput, calls=%fused_computation.24 | convolution fusion | flops 1990656 | bytes 405504 | tf_op jit(solution)/shard_map/kaon,kcon->acon/dot_general | solution.py:59
  278.4 8.7 %fusion.12 = bf16[9,3,8,128]{0,1,3,2:T(4,128)(2,1)S(1)} fusion(f32[2,3,8,128]{1,0,3,2:T(2,128)S(1)} %copy.208, f32[2,9,8,128]{1,0,3,2:T(2,128)S(1)} %copy.201), kind=kOutput, calls=%fused_computation.36 | convolution fusion | flops 691200 | bytes 153600 | tf_op jit(solution)/shard_map/kaon,kbon->abon/dot_general | solution.py:50
  287.2 8.6 %pad_maximum_fusion.1 = bf16[9,3,8,640]{0,1,3,2:T(4,128)(2,1)} fusion(bf16[9,3,8,128]{0,1,3,2:T(4,128)(2,1)S(1)} %fusion.12, bf16[9,3,8,512]{0,1,3,2:T(4,128)(2,1)} %copy-done.6), kind=kLoop, calls=%fused_computation.7 | loop fusion | flops 138240 | bytes 552960 | tf_op jit(solution)/shard_map/concatenate | solution.py:139
  312.2 10.6 %convolution_bitcast_fusion.2 = bf16[256,9,3,640]{0,1,2,3:T(8,128)(2,1)} fusion(bf16[9,3,8,640]{0,1,2,3:T(4,128)(2,1)} %pad_maximum_fusion, s32[8,640]{0,1:T(8,128)S(1)} %copy.214), kind=kOutput, calls=%fused_computation.5 | convolution fusion | flops 72089600 | bytes 9144320 | tf_op jit(solution)/shard_map/iop,abop->iabp/dot_general | solution.py:89
  322.8 36.4 %copy.216 = bf16[256,9,3,640]{3,2,1,0:T(4,128)(2,1)} copy(bf16[256,9,3,640]{0,1,2,3:T(8,128)(2,1)} %convolution_bitcast_fusion.2) | data formatting | bytes 17694720 | tf_op jit(solution)/shard_map/iop,abop->iabp/transpose | solution.py:89
  359.2 9.3 %copy.267 = bf16[288,8,3,640]{3,1,2,0:T(8,128)(2,1)} copy(bf16[288,8,3,640]{3,2,1,0:T(4,128)(2,1)} %bitcast.323) | data formatting | bytes 17694720
  368.5 10.6 %convolution_bitcast_fusion.1 = bf16[256,9,3,640]{0,1,2,3:T(8,128)(2,1)} fusion(bf16[9,3,8,640]{0,1,3,2:T(4,128)(2,1)} %pad_maximum_fusion.1, s32[8,640]{0,1:T(8,128)S(1)} %copy.214), kind=kOutput, calls=%fused_computation.4 | convolution fusion | flops 72089600 | bytes 9144320 | tf_op jit(solution)/shard_map/iop,abop->iabp/dot_general | solution.py:89
  379.1 36.5 %copy.218 = bf16[256,9,3,640]{3,2,1,0:T(4,128)(2,1)} copy(bf16[256,9,3,640]{0,1,2,3:T(8,128)(2,1)} %convolution_bitcast_fusion.1) | data formatting | bytes 17694720 | tf_op jit(solution)/shard_map/iop,abop->iabp/transpose | solution.py:89
  415.7 9.4 %copy.268 = bf16[288,8,3,640]{3,1,2,0:T(8,128)(2,1)} copy(bf16[288,8,3,640]{3,2,1,0:T(4,128)(2,1)} %bitcast.324) | data formatting | bytes 17694720
  429.7 29.2 %fusion.128 = f32[2304,2304]{1,0:T(8,128)} fusion(bf16[2304,1920]{1,0:T(8,128)(2,1)} %bitcast.325, bf16[2304,1920]{1,0:T(8,128)(2,1)} %bitcast.326), kind=kOutput, calls=%fused_computation.301 | convolution fusion | flops 20384317440 | bytes 38928384 | tf_op jit(solution)/shard_map/rk,ck->rc/dot_general | solution.py:96
  460.9 52.7 %all-reduce.6.cloned.1.call-done = f32[90,256]{0,1:T(8,128)} async-done(((f32[90,256]{0,1:T(8,128)}), f32[90,256]{0,1:T(8,128)}) %all-reduce.6.cloned.1.call-update) | async-done | bytes 92176
  515.6 9.4 %broadcast_multiply_fusion = f32[16,9,256,9]{3,2,1,0:T(8,128)} fusion(f32[16,256]{1,0:T(8,128)S(1)} %fusion.110, f32[16,9,9]{2,1,0:T(8,128)S(1)} %copy.213), kind=kLoop, calls=%fused_computation.3 | loop fusion | flops 331776 | bytes 1348672 | tf_op jit(solution)/shard_map/mul | solution.py:166
  525.0 13.4 %mul.755 = f32[144,2304]{1,0:T(8,128)S(1)} reshape(f32[16,9,256,9]{3,2,1,0:T(8,128)} %broadcast_multiply_fusion) | data formatting | bytes 2654208 | tf_op jit(solution)/shard_map/mul | solution.py:166
  538.4 111.7 %reduce-scatter.2.cloned.1.call-done = f32[144,2304]{1,0:T(8,128)} async-done(((f32[2304,2304]{1,0:T(8,128)}), f32[144,2304]{1,0:T(8,128)}) %reduce-scatter.2.cloned.1.call-update) | async-done | bytes 1327120 | tf_op jit(solution)/shard_map/reduce_scatter | solution.py:145
  652.0 11.7 %custom-call.20 = f32[1,128,128]{2,1,0:T(8,128)S(1)} custom-call(f32[1,128,128]{2,1,0:T(8,128)S(1)} %cholesky.123), custom_call_target="Cholesky" | custom-call | tf_op jit(solution)/shard_map/jit(cholesky)/cholesky | solution.py:174
  664.4 9.8 %custom-call.21 = f32[1,1,128,128]{2,3,1,0:T(8,128)S(1)} custom-call(f32[1,1,128,128]{3,2,1,0:T(8,128)S(1)} %get-tuple-element.75), custom_call_target="InvertDiagBlocksLowerTriangular" | custom-call | tf_op jit(solution)/shard_map/jit(cholesky)/cholesky | solution.py:174
  678.2 19.7 %custom-call.23 = f32[2,128,128]{1,2,0:T(8,128)S(1)} custom-call(f32[2,128,128]{2,1,0:T(8,128)S(1)} %pad_maximum_fusion.3), custom_call_target="InvertDiagBlocksLowerTriangular" | custom-call | tf_op jit(solution)/shard_map/jit(_cho_solve)/triangular_solve | solution.py:175
  (180 shorter events, 106.8 us)
Async XLA Ops:
  7.2 0.8 copy-start
  31.0 0.7 copy-start.2
  31.7 23.1 %copy-start.14 = (s32[8,512]{1,0:T(8,128)S(1)}, s32[8,512]{1,0:T(8,128)}, u32[]{:S(2)}) copy-start(s32[8,512]{1,0:T(8,128)} %param.12) | copy-start | bytes 49156
  31.7 23.1 %copy-start.16 = (s32[512]{0:T(512)S(1)}, s32[512]{0:T(512)}, u32[]{:S(2)}) copy-start(s32[512]{0:T(512)} %param.13) | copy-start | bytes 6148
  31.7 24.7 %copy-start.15 = (bf16[2,8,512]{2,1,0:T(8,128)(2,1)S(1)}, bf16[2,8,512]{2,1,0:T(8,128)(2,1)}, u32[]{:S(2)}) copy-start(bf16[2,8,512]{2,1,0:T(8,128)(2,1)} %param.11) | copy-start | bytes 49156
  31.7 24.7 %copy-start.13 = (bf16[6,8,512]{2,1,0:T(8,128)(2,1)S(1)}, bf16[6,8,512]{2,1,0:T(8,128)(2,1)}, u32[]{:S(2)}) copy-start(bf16[6,8,512]{2,1,0:T(8,128)(2,1)} %param.10) | copy-start | bytes 147460
  31.7 24.7 %copy-start.10 = (bf16[18,8,512]{2,1,0:T(8,128)(2,1)S(1)}, bf16[18,8,512]{2,1,0:T(8,128)(2,1)}, u32[]{:S(2)}) copy-start(bf16[18,8,512]{2,1,0:T(8,128)(2,1)} %param.9) | copy-start | bytes 442372
  58.1 180.2 %all-to-all-start = ((bf16[8,2,1728]{2,1,0:T(2,128)(2,1)}), bf16[8,2,1728]{2,1,0:T(2,128)(2,1)S(1)}, u32[]{:S(2)}, u32[]{:S(2)}) async-start(bf16[8,2,1728]{2,1,0:T(2,128)(2,1)} %reshape.1177), calls=%async_computation | async-start | bytes 114688 | tf_op jit(solution)/shard_map/all_to_all | solution.py:127
  63.4 450.2 %all-reduce.6.cloned.1.call-start = ((), (), s32[]{:S(2)}) async-start(), calls=%async_computation.3 | async-start | bytes 262144
  105.6 57.6 %copy-start.3 = (f32[2,9,8,512]{1,0,3,2:T(2,128)S(1)}, f32[2,9,8,512]{1,0,3,2:T(2,128)}, u32[]{:S(2)}) copy-start(f32[2,9,8,512]{1,0,3,2:T(2,128)} %copy.189) | copy-start | bytes 884740
  105.6 57.6 %copy-start.7 = (f32[2,3,8,512]{1,0,3,2:T(2,128)S(1)}, f32[2,3,8,512]{1,0,3,2:T(2,128)}, u32[]{:S(2)}) copy-start(f32[2,3,8,512]{1,0,3,2:T(2,128)} %copy.194) | copy-start | bytes 294916
  197.3 7.6 %copy-start.6 = (bf16[9,3,8,512]{0,1,3,2:T(4,128)(2,1)}, bf16[9,3,8,512]{0,1,3,2:T(4,128)(2,1)S(1)}, u32[]{:S(2)}) copy-start(bf16[9,3,8,512]{0,1,3,2:T(4,128)(2,1)S(1)} %fusion.9) | copy-start | bytes 663556
  204.9 1.9 copy-start.4
  266.7 11.6 %copy-start.11 = (f32[8,128,1,9]{3,2,1,0:T(1,128)S(1)}, f32[8,128,1,9]{3,2,1,0:T(1,128)}, u32[]{:S(2)}) copy-start(f32[8,128,1,9]{3,2,1,0:T(1,128)} %fusion.23) | copy-start | bytes 110596
  287.2 11.5 %copy-start.5 = (bf16[9,3,8,512]{0,1,2,3:T(4,128)(2,1)S(1)}, bf16[9,3,8,512]{0,1,2,3:T(4,128)(2,1)}, u32[]{:S(2)}) copy-start(bf16[9,3,8,512]{0,1,2,3:T(4,128)(2,1)} %copy-done.4) | copy-start | bytes 663556
  298.7 6.3 copy-start.19
  415.7 9.7 %copy-start.17 = (s32[128]{0:T(128)S(1)}, s32[128]{0:T(128)}, u32[]{:S(2)}) copy-start(s32[128]{0:T(128)} %get-tuple-element.95) | copy-start | bytes 1540
  415.7 12.5 %copy-start.9 = (f32[90,1,512]{2,1,0:T(1,128)S(1)}, f32[90,1,512]{2,1,0:T(1,128)}, u32[]{:S(2)}) copy-start(f32[90,1,512]{2,1,0:T(1,128)} %get-tuple-element.48) | copy-start | bytes 552964
  415.7 12.5 %copy-start.12 = (f32[90,256]{0,1:T(8,128)S(1)}, f32[90,256]{0,1:T(8,128)}, u32[]{:S(2)}) copy-start(f32[90,256]{0,1:T(8,128)} %convolution_add_fusion.1) | copy-start | bytes 276484
  429.6 220.4 %reduce-scatter.2.cloned.1.call-start = ((), (), s32[]{:S(2)}) async-start(), calls=%async_computation.2 | async-start | bytes 22560768 | tf_op jit(solution)/shard_map/reduce_scatter | solution.py:145
  458.9 0.7 copy-start.18
  525.0 174.5 %copy-start.1 = (s32[2048]{0:T(1024)S(1)}, s32[2048]{0:T(1024)}, u32[]{:S(2)}) copy-start(s32[2048]{0:T(1024)} %param.15) | copy-start | bytes 24580
  651.6 47.8 %copy-start.8 = (f32[144,2304]{1,0:T(8,128)}, f32[144,2304]{1,0:T(8,128)S(1)}, u32[]{:S(2)}) copy-start(f32[144,2304]{1,0:T(8,128)S(1)} %sub.277) | copy-start | bytes 3981316
Sparse Core Ops, SparseCore 0:
  429.8 83.8 all-reduce.5
  517.5 132.5 reduce-scatter.1
where the time goes:
time: 711 us; the launch traced here: 706 us
  matrix products  218 us (31%)
  local copies, waits for them, and re-layouts  194 us (27%)
  waiting for transfers between devices  164 us (23%)
  other arithmetic  107 us (15%)
  between operations  17.2 us (2%)
    reduce_scatter x1, waiting for transfers between devices, per_device(): lax.psum_scatter(schur_rows(camera_point_coupling, reduced_camera_matrix,...  112 us
    dot_general x2, matrix products, eliminate(): jnp.einsum('kaon,kcon->acon', camera_rows, camera_rows, precision=EXACT_P...  73.6 us
    transpose x2, local copies, waits for them, and re-layouts, place_blocks(): jnp.einsum('iop,abop->iabp', onehot, values, preferred_element_type=jnp.b...  73 us
    unnamed x3, waiting for transfers between devices  52.8 us
    dot_general x2, matrix products, eliminate(): jnp.einsum('kaon,kbon->abon', camera_rows, point_rows, precision=EXACT_PR...  42.8 us
    dot_general x1, matrix products, schur_rows(): jnp.einsum('rk,ck->rc', left_side, right_side, preferred_element_type=jnp...  29.2 us
    unnamed x49, local copies, waits for them, and re-layouts  24.9 us
    another operation x7, other arithmetic, per_device(): factor = jnp.linalg.cholesky(diagonal)  24.4 us
  transfers between devices with their start and end apart: 3, of which 2 were waited for; matrix products, arithmetic and copies ran while one was open for 32% of the time, Pallas kernels for 0%

commit v1 on v0

v1 whole, which is shorter than its diff:
```python
import jax
import jax.numpy as jnp
from jax import lax
from jax.experimental import pallas as pl
from jax.experimental.pallas import tpu as pltpu
from jax.sharding import PartitionSpec as P

CAMS = 256
OWN = 16
OBS = 8
PTS = 512
FAR = 128
ALL = PTS + FAR
CAP = 256
ROWS = 224
SLOT = 208
COUNT = 216
OVER = 217
ROUNDS = -(-ALL // CAP)
DAMPING = 0.5
EXACT = lax.Precision.HIGHEST
F32 = jnp.float32
BF16 = jnp.bfloat16
NT = (((1,), (1,)), ((), ()))
VMEM_BYTES = 56 * 1024 * 1024


def iota(shape, dim):
    return lax.broadcasted_iota(jnp.int32, shape, dim)


def running_count(hits):
    tri = (iota((128, 128), 0) <= iota((128, 128), 1)).astype(BF16)
    parts = []
    base = jnp.zeros((hits.shape[0], 1), F32)
    for t in range(hits.shape[1] // 128):
        part = hits[:, t * 128 : (t + 1) * 128]
        parts.append(jnp.dot(part.astype(BF16), tri, preferred_element_type=F32) + base)
        base = base + jnp.sum(part, axis=1, keepdims=True)
    return jnp.concatenate(parts, axis=1)


def sort_out_kernel(cam_ref, pt_ref, res_ref, oc_ref, cnt_ref, ncl_ref, nsl_ref, slot_ref, far_ref):
    ids = oc_ref[...]
    cluster = ids >> 8
    old = cluster[0:1, 0:128]
    code = ncl_ref[...] * CAMS + nsl_ref[...]
    row = iota((16, 128), 0)
    tables = [
        jnp.sum(jnp.where(row == 2 * old + t, code, 0), axis=0, keepdims=True) for t in range(2)
    ]
    tables = [jnp.broadcast_to(t, (OBS, 128)) for t in tables]
    found = []
    for t in range(PTS // 128):
        local = ids[:, t * 128 : (t + 1) * 128] & 255
        lane = local & 127
        low, high = [
            jnp.take_along_axis(table, lane, axis=1, mode="promise_in_bounds") for table in tables
        ]
        found.append(jnp.where(local < 128, low, high))
    found = jnp.concatenate(found, axis=1)
    aim = found >> 8
    place = (found & 255) + 1
    live = iota((OBS, PTS), 0) < cnt_ref[...]
    home = jnp.where(live & (aim == cluster), place, 0)
    abroad = live & (aim != cluster)
    away = jnp.where(abroad, place, 0)
    slot_ref[0:8, :] = home.astype(F32).astype(BF16)
    slot_ref[8:16, :] = jnp.zeros((8, PTS), BF16)
    target = jnp.max(jnp.where(abroad, aim, -1), axis=0, keepdims=True)
    hits = (jnp.broadcast_to(target, (8, PTS)) == iota((8, PTS), 0)).astype(F32)
    rank = jnp.sum((running_count(hits) - 1.0) * hits, axis=0, keepdims=True)
    column = jnp.where(target >= 0, target * 16 + rank.astype(jnp.int32), -1)
    chooser = (jnp.broadcast_to(column, (FAR, PTS)) == iota((FAR, PTS), 0)).astype(BF16)
    mask = abroad.astype(F32)
    mask2 = jnp.concatenate([mask, mask], axis=0).astype(BF16)

    def send(ref, groups):
        rows = jnp.concatenate([ref[16 * g : 16 * g + 16, :] * mask2 for g in range(groups)], axis=0)
        return lax.dot_general(chooser, rows, NT, preferred_element_type=F32)

    far_ref[:, 0:208] = jnp.concatenate(
        [send(cam_ref, 9), send(pt_ref, 3), send(res_ref, 1)], axis=1
    ).astype(BF16)
    slots = jnp.concatenate([away.astype(F32), jnp.zeros((40, PTS), F32)], axis=0).astype(BF16)
    far_ref[:, 208:256] = lax.dot_general(
        chooser, slots, NT, preferred_element_type=F32
    ).astype(BF16)


def pack_kernel(first_rank, cam_ref, pt_ref, res_ref, slot_ref, far_ref, out_ref, feat):
    feat[0:144, 0:PTS] = cam_ref[...]
    feat[144:192, 0:PTS] = pt_ref[...]
    feat[192:208, 0:PTS] = res_ref[...]
    feat[208:224, 0:PTS] = slot_ref[...]
    feat[:, PTS:ALL] = far_ref[...].astype(F32).T[0:ROWS, :].astype(BF16)
    slots = feat[208:224, :].astype(F32)[0:8, :].astype(jnp.int32)
    owner = ((slots + 15) >> 4) - 1
    member = iota((16, ALL), 0)
    touch = jnp.zeros((16, ALL), jnp.bool_)
    for o in range(OBS):
        touch = touch | (jnp.broadcast_to(owner[o : o + 1, :], (16, ALL)) == member)
    hits = touch.astype(F32)
    count = running_count(hits)
    total = jnp.max(count, axis=1, keepdims=True)
    rank = count - 1.0 - first_rank
    rank = jnp.where(touch & (rank >= 0.0) & (rank < CAP), rank, -1.0)
    over = jnp.max((total > CAP).astype(F32), axis=0, keepdims=True)
    seat = iota((CAP, ALL), 0).astype(F32)
    here = jnp.clip(total - first_rank, 0.0, float(CAP))
    line = iota((16, CAP), 0)
    for d in range(16):
        chosen = (jnp.broadcast_to(rank[d : d + 1, :], (CAP, ALL)) == seat).astype(BF16)
        moved = lax.dot_general(feat[...], chosen, NT, preferred_element_type=F32)
        out_ref[d, 0:208, :] = moved[0:208, :].astype(BF16)
        tail = jnp.where(
            line < 8,
            moved[208:224, :],
            jnp.where(line == 8, here[d : d + 1, :], jnp.where(line == 9, over, 0.0)),
        )
        out_ref[d, 208:224, :] = tail.astype(BF16)


def block_values(f):
    slot = f[SLOT : SLOT + 8, :]
    valid = slot > 0.0
    cam = [[f[(k * 9 + a) * 8 : (k * 9 + a) * 8 + 8, :] for a in range(9)] for k in range(2)]
    pt = [
        [
            jnp.where(valid, f[144 + (k * 3 + b) * 8 : 152 + (k * 3 + b) * 8, :], 0.0)
            for b in range(3)
        ]
        for k in range(2)
    ]
    res = [jnp.where(valid, f[192 + k * 8 : 200 + k * 8, :], 0.0) for k in range(2)]

    def over_obs(x):
        return jnp.sum(x, axis=0, keepdims=True)

    v = {}
    for b in range(3):
        for c in range(b, 3):
            v[b, c] = over_obs(pt[0][b] * pt[0][c] + pt[1][b] * pt[1][c]) + (
                DAMPING if b == c else 0.0
            )
            v[c, b] = v[b, c]
    g = [over_obs(pt[0][b] * res[0] + pt[1][b] * res[1]) for b in range(3)]

    def cofactor(i, j):
        r = [x for x in range(3) if x != i]
        c = [x for x in range(3) if x != j]
        minor = v[r[0], c[0]] * v[r[1], c[1]] - v[r[0], c[1]] * v[r[1], c[0]]
        return minor if (i + j) % 2 == 0 else -minor

    cof = {(i, j): cofactor(i, j) for i in range(3) for j in range(i, 3)}
    det = v[0, 0] * cof[0, 0] + v[0, 1] * cof[0, 1] + v[0, 2] * cof[0, 2]
    inv = {}
    for i in range(3):
        for j in range(i, 3):
            inv[i, j] = cof[i, j] / det
            inv[j, i] = inv[i, j]
    w = {}
    z = {}
    for a in range(9):
        for b in range(3):
            w[a, b] = (cam[0][a] * pt[0][b] + cam[1][a] * pt[1][b]).astype(BF16).astype(F32)
        for b in range(3):
            z[a, b] = w[a, 0] * inv[0, b] + w[a, 1] * inv[1, b] + w[a, 2] * inv[2, b]
    return slot, cam, res, w, z, g


def system_kernel(
    blocks, m_ref, x_ref, out_ref, step_ref, wv, wp, zp, ap, gp, acc, acc_u, acc_g, turned, dm, st, woven
):
    m = m_ref[0]
    acc[...] = jnp.zeros_like(acc)
    acc_u[...] = jnp.zeros_like(acc_u)
    acc_g[...] = jnp.zeros_like(acc_g)
    gp[...] = jnp.zeros_like(gp)
    names = (iota((16, 128), 0) + 1).astype(F32).astype(BF16)

    def spread(row):
        return jnp.broadcast_to(row, (16, 128)).astype(BF16)

    def choose(slots, own, values):
        out = jnp.zeros((16, 128), BF16)
        for o in range(OBS):
            out = jnp.where(slots[o] == own, values[o], out)
        return out

    def chunk(s, carry):
        slot, cam, res, w, z, g = block_values(x_ref[s].astype(F32))
        for a in range(9):
            for b in range(3):
                wv[(a * 3 + b) * 8 : (a * 3 + b) * 8 + 8, :] = w[a, b]
        for b in range(3):
            high = g[b].astype(BF16)
            rest = g[b] - high.astype(F32)
            mid = rest.astype(BF16)
            low = (rest - mid.astype(F32)).astype(BF16)
            rows = jnp.concatenate(
                [high.astype(F32), mid.astype(F32), low.astype(F32), jnp.zeros((13, CAP), F32)], axis=0
            )
            gp[:, b * CAP : (b + 1) * CAP] = rows.astype(BF16)
        mine = ((iota((16, 128), 0) + 1) + m * OWN).astype(F32).astype(BF16)
        for h in range(2):
            lanes = slice(h * 128, h * 128 + 128)
            slots = [spread(slot[o : o + 1, lanes]) for o in range(OBS)]

            def own(value):
                return choose(slots, mine, [spread(value[o : o + 1, lanes]) for o in range(OBS)])

            for a in range(9):
                for b in range(3):
                    zp[a * 16 : a * 16 + 16, b * CAP + h * 128 : b * CAP + h * 128 + 128] = own(
                        z[a, b]
                    )
                for k in range(2):
                    ap[a * 16 : a * 16 + 16, k * CAP + h * 128 : k * CAP + h * 128 + 128] = own(
                        cam[k][a]
                    )
            for k in range(2):
                ap[144:160, k * CAP + h * 128 : k * CAP + h * 128 + 128] = own(res[k])
        acc_u[...] += lax.dot_general(ap[...], ap[0:144, :], NT, preferred_element_type=F32)
        acc_g[...] += lax.dot_general(gp[...], zp[...], NT, preferred_element_type=F32)
        for a in range(9):
            for h in range(2):
                lanes = slice(h * 128, h * 128 + 128)
                slots = [spread(slot[o : o + 1, lanes]) for o in range(OBS)]
                values = [
                    [
                        spread(wv[(a * 3 + b) * 8 + o : (a * 3 + b) * 8 + o + 1, lanes])
                        for o in range(OBS)
                    ]
                    for b in range(3)
                ]
                for t in range(16):
                    here = names + jnp.asarray(16 * t, BF16)
                    outs = [jnp.zeros((16, 128), BF16)] * 3
                    for o in range(OBS):
                        same = slots[o] == here
                        outs = [jnp.where(same, values[b][o], outs[b]) for b in range(3)]
                    for b in range(3):
                        wp[
                            a * CAMS + t * 16 : a * CAMS + t * 16 + 16,
                            b * CAP + h * 128 : b * CAP + h * 128 + 128,
                        ] = outs[b]
            acc[a] += lax.dot_general(
                wp[a * CAMS : (a + 1) * CAMS, :], zp[...], NT, preferred_element_type=F32
            )
        return carry

    lax.fori_loop(0, blocks, chunk, 0)

    rows_u = iota((144, 144), 0)
    cols_u = iota((144, 144), 1)
    block = jnp.where((rows_u & 15) == (cols_u & 15), acc_u[0:144, :], 0.0) + jnp.where(
        rows_u == cols_u, DAMPING, 0.0
    )
    grad = jnp.sum(
        jnp.where(iota((16, 144), 0) == (iota((16, 144), 1) & 15), acc_u[144:160, :], 0.0),
        axis=0,
        keepdims=True,
    ) - jnp.sum(acc_g[...], axis=0, keepdims=True)
    dm[...] = jnp.zeros_like(dm)
    own_rows = pl.ds(pl.multiple_of(m * OWN, OWN), OWN)
    for a in range(9):
        acc[a] = -acc[a]
        acc[a, own_rows, :] += block[a * 16 : a * 16 + 16, :]
        dm[a * 16 : a * 16 + 16, 0:144] = acc[a, own_rows, :]
    dm[144:145, 0:144] = grad
    for a in range(9):
        turned[pl.ds(a, CAMS, stride=9), 0:128] = acc[a, :, 0:128]
        st[pl.ds(a, CAMS, stride=9), :] = jnp.concatenate(
            [acc[a, :, 128:144], jnp.zeros((CAMS, 112), F32)], axis=1
        )
    for t in range(18):
        lanes = slice(t * 128, t * 128 + 128)
        first = turned[lanes, :].T
        for a in range(8):
            woven[pl.ds(t * 144 + a, 16, stride=9), :] = first[a * 16 : a * 16 + 16, :]
        woven[pl.ds(t * 144 + 8, 16, stride=9), :] = st[lanes, :].T[0:16, :]
        out_ref[:, lanes] = woven[t * 144 : t * 144 + 144, :]

    whole = dm[...]
    flipped = whole.T
    lane = iota((144, 256), 1)
    mat = jnp.where(lane < 144, 0.5 * (whole[0:144, :] + flipped[0:144, :]), flipped[0:144, :])
    sub = iota((144, 1), 0)
    left, right = mat[:, 0:128], mat[:, 128:256]
    for k in range(144):
        if k < 128:
            col = left[:, k : k + 1]
        else:
            col = right[:, k - 128 : k - 127]
        scale = 1.0 / col[k : k + 1, :]
        new_right = right[k : k + 1, :] * scale
        less = col - (sub == k).astype(F32)
        if k < 128:
            left = left - less * (left[k : k + 1, :] * scale)
        right = right - less * new_right
    step = jnp.broadcast_to(-right[:, 16:17], (144, 128))
    for a in range(9):
        st[pl.ds(a, 16, stride=9), :] = step[a * 16 : a * 16 + 16, :]
    step_ref[...] = st[0:256, :].T[0:8, :]


def per_device(cam_jac, point_jac, residuals, obs_camera, obs_count, new_cluster, new_slot):
    params = pltpu.CompilerParams(vmem_limit_bytes=VMEM_BYTES)
    vmem = pl.BlockSpec(memory_space=pltpu.VMEM)
    cam = cam_jac.reshape(144, PTS)
    pt = point_jac.reshape(48, PTS)
    res = residuals.reshape(16, PTS)
    slots, far = pl.pallas_call(
        sort_out_kernel,
        out_shape=(jax.ShapeDtypeStruct((16, PTS), BF16), jax.ShapeDtypeStruct((FAR, 256), BF16)),
        in_specs=[vmem] * 7,
        out_specs=(vmem, vmem),
        compiler_params=params,
        name="sort_out",
    )(
        cam,
        pt,
        res,
        obs_camera,
        obs_count.reshape(1, PTS),
        new_cluster.reshape(16, 128),
        new_slot.reshape(16, 128),
    )
    far = lax.all_to_all(
        far.reshape(8, 16, 256), "cluster", split_axis=0, concat_axis=0, tiled=True
    ).reshape(FAR, 256)

    def packed(turn):
        def body(*refs):
            pack_kernel(float(turn * CAP), *refs)

        sent = pl.pallas_call(
            body,
            out_shape=jax.ShapeDtypeStruct((16, ROWS, CAP), BF16),
            in_specs=[vmem] * 5,
            out_specs=vmem,
            scratch_shapes=[pltpu.VMEM((ROWS, ALL), BF16)],
            compiler_params=params,
            name="pack",
        )(cam, pt, res, slots, far)
        return lax.all_to_all(sent, "member", split_axis=0, concat_axis=0, tiled=True)

    def system(blocks):
        count = blocks.shape[0]

        def body(*refs):
            system_kernel(count, *refs)

        return pl.pallas_call(
            body,
            out_shape=(
                jax.ShapeDtypeStruct((144, 9 * CAMS), F32),
                jax.ShapeDtypeStruct((8, 256), F32),
            ),
            in_specs=[pl.BlockSpec(memory_space=pltpu.SMEM), vmem],
            out_specs=(vmem, vmem),
            scratch_shapes=[
                pltpu.VMEM((216, CAP), F32),
                pltpu.VMEM((9 * CAMS, 3 * CAP), BF16),
                pltpu.VMEM((144, 3 * CAP), BF16),
                pltpu.VMEM((160, 2 * CAP), BF16),
                pltpu.VMEM((16, 3 * CAP), BF16),
                pltpu.VMEM((9, CAMS, 144), F32),
                pltpu.VMEM((160, 144), F32),
                pltpu.VMEM((16, 144), F32),
                pltpu.VMEM((9 * CAMS, 128), F32),
                pltpu.VMEM((256, 256), F32),
                pltpu.VMEM((9 * CAMS, 128), F32),
                pltpu.VMEM((18 * 144, 128), F32),
            ],
            compiler_params=params,
            name="system",
        )(lax.axis_index("member").astype(jnp.int32).reshape(1), blocks)

    arrived = packed(0)

    def more_rounds(arrived):
        return system(jnp.concatenate([arrived] + [packed(t) for t in range(1, ROUNDS)], axis=0))

    matrix, step = lax.cond(jnp.max(arrived[:, OVER, 0]) > 0, more_rounds, system, arrived)
    return matrix, step[0, 0:144]


def solution(mesh):
    in_specs = (
        P(None, None, ("cluster", "member")),
        P(None, None, ("cluster", "member")),
        P(None, None, ("cluster", "member")),
        P(None, ("cluster", "member")),
        P(("cluster", "member")),
        P(),
        P(),
    )
    out_specs = (P(("cluster", "member"), None), P(("cluster", "member")))
    return jax.shard_map(
        per_device, mesh=mesh, in_specs=in_specs, out_specs=out_specs, check_vma=False
    )
```

time: 711 us -> 119 us (0.17)
  matrix products: 218 us -> 0 us
  local copies, waits for them, and re-layouts: 194 us -> 1.27 us
  waiting for transfers between devices: 164 us -> 0 us
  other arithmetic: 107 us -> 0.62 us
  Pallas kernels: 0 us -> 71.7 us
  blocking collectives: 0 us -> 43.7 us
  between operations: 17.2 us -> 1.32 us
    dot_general x33 -> x0, matrix products: 217 us -> none  [the longest x2 73.6 us: eliminate(): jnp.einsum('kaon,kcon->acon', camera_rows, camera_rows, precision=EXACT_P...]
    reduce_scatter x1 -> x0, waiting for transfers between devices: 112 us -> none  [per_device(): lax.psum_scatter(schur_rows(camera_point_coupling, reduced_camera_matrix,...]
    transpose x6 -> x0, local copies, waits for them, and re-layouts: 94.4 us -> none  [the longest x2 73 us: place_blocks(): jnp.einsum('iop,abop->iabp', onehot, values, preferred_element_type=jnp.b...]
    pallas_call x0 -> x3, Pallas kernels: none -> 71.7 us  [the longest x1 65.5 us: system(): pl.pallas_call(body, out_shape=(jax.ShapeDtypeStruct((144, 9 * CAMS), F32...]
    unnamed x3 -> x0, waiting for transfers between devices: 52.8 us -> none
    gather x4 -> x0, local copies, waits for them, and re-layouts: 46.1 us -> none  [the longest x2 23 us: per_device(): row_of = jnp.take(new_slot, obs_camera)]
    another operation x19 -> x0, other arithmetic: 45.5 us -> none  [the longest x7 24.4 us: per_device(): factor = jnp.linalg.cholesky(diagonal)]
    all_to_all x0 -> x2, blocking collectives: none -> 43.7 us  [the longest x1 32.7 us: packed(): lax.all_to_all(sent, 'member', split_axis=0, concat_axis=0, tiled=True)]
  transfers between devices with their start and end apart: 3 -> 0, of which waited for: 2 -> 0; matrix products, arithmetic and copies ran while one was open for 32% -> 0% of each run, Pallas kernels for 0% -> 0%
where the time goes in v1:
time: 119 us
  Pallas kernels  71.7 us (60%)
  blocking collectives  43.7 us (37%)
  between operations  1.32 us (1%)
  local copies, waits for them, and re-layouts  1.27 us (1%)
    pallas_call x1, Pallas kernels, system(): pl.pallas_call(body, out_shape=(jax.ShapeDtypeStruct((144, 9 * CAMS), F32...  65.5 us
    all_to_all x1, blocking collectives, packed(): lax.all_to_all(sent, 'member', split_axis=0, concat_axis=0, tiled=True)  32.7 us
    all_to_all x1, blocking collectives, per_device(): lax.all_to_all(far.reshape(8, 16, 256), 'cluster', split_axis=0, concat_a...  11 us
    pallas_call x1, Pallas kernels, packed(): pl.pallas_call(body, out_shape=jax.ShapeDtypeStruct((16, ROWS, CAP), BF16...  4.1 us

profile of v1, /device:TPU:0, one launch (start us, length us, event | category | flops | bytes accessed | tf_op | source)
XLA Modules:
  0.0 118.8 jit_solution(7201881402105332871)
XLA Ops:
  0.6 2.2 %sort_out.1 = (bf16[16,512]{1,0:T(8,128)(2,1)S(1)}, bf16[128,256]{1,0:T(8,128)(2,1)}) custom-call(bf16[144,512]{1,0:T(8,128)(2,1)} %bitcast.12, bf16[48,512]{1,0:T(8,128)(2,1)} %bitcast.17, bf16[16,512]{1,0:T(8,128)(2,1)} %bitcast.20, s32[8,512]{1,0:T(8,128)} %oc_ref.1, s32[1,512]{1,0:T(1,128)} %bitcast.26, s32[16,128]{1,0:T(8,128)} %bitcast.24, ...), custom_call_target="tpu_custom_call" | custom-call | tf_op jit(solution)/shard_map/sort_out/pallas_call | solution.py:314
  2.8 11.0 %all_to_all.21 = bf16[8,16,256]{2,1,0:T(8,128)(2,1)S(1)} all-to-all(bf16[8,16,256]{2,1,0:T(8,128)(2,1)} %bitcast.23), channel_id=1, replica_groups=mesh['cluster'=8,'member'=16] {'cluster'}, dimensions={0} | all-to-all | bytes 131072 | tf_op jit(solution)/shard_map/all_to_all | solution.py:330
  13.8 4.1 %pack.5 = bf16[16,224,256]{2,1,0:T(8,128)(2,1)} custom-call(bf16[144,512]{1,0:T(8,128)(2,1)} %bitcast.13, bf16[48,512]{1,0:T(8,128)(2,1)} %bitcast.18, bf16[16,512]{1,0:T(8,128)(2,1)} %bitcast.21, bf16[16,512]{1,0:T(8,128)(2,1)S(1)} %get-tuple-element.32.refs_3_, bf16[128,256]{1,0:T(8,128)(2,1)S(1)} %bitcast.15), custom_call_target="tpu_custom_call" | custom-call | tf_op jit(solution)/shard_map/pack/pallas_call | solution.py:338
  17.9 0.0 copy-start
  17.9 0.0 copy-start.1
  17.9 0.0 copy-start.2
  17.9 32.7 %all_to_all.22 = bf16[16,224,256]{2,1,0:T(8,128)(2,1)S(1)} all-to-all(bf16[16,224,256]{2,1,0:T(8,128)(2,1)} %pack.5), channel_id=1, replica_groups=mesh['cluster'=8,'member'=16] {'member'}, dimensions={0} | all-to-all | bytes 3670016 | tf_op jit(solution)/shard_map/all_to_all | solution.py:347
  50.6 0.6 slice_reduce_fusion
  51.9 0.0 copy-done
  51.9 0.0 copy-done.1
  51.9 0.0 copy-done.2
  51.9 66.9 %conditional.1 = (f32[144,2304]{1,0:T(8,128)}, f32[144]{0:T(256)}) conditional(s32[]{:T(128)} %convert_element_type.3, bf16[16,224,256]{2,1,0:T(8,128)(2,1)S(1)} %all_to_all.22, (bf16[144,512]{1,0:T(8,128)(2,1)S(1)}, bf16[48,512]{1,0:T(8,128)(2,1)S(1)}, bf16[16,512]{1,0:T(8,128)(2,1)S(1)}, bf16[16,512]{1,0:T(8,128)(2,1)S(1)}, ...), branch_computations={%region_1.0_spmd, %region_2.0_spmd} | conditional | flops 5505026 | bytes 22021348 | solution.py:386
  52.1 65.5 %system.2 = (f32[144,2304]{1,0:T(8,128)}, f32[8,256]{1,0:T(8,128)}) custom-call(s32[1]{0:T(128)} %bitcast.refs_0_, bf16[16,224,256]{2,1,0:T(8,128)(2,1)S(1)} %refs_1_), custom_call_target="tpu_custom_call" | custom-call | tf_op jit(solution)/shard_map/cond/branch_0_fun/system/pallas_call | solution.py:355
  117.6 1.3 %slice.7 = f32[1,144]{1,0:T(1,128)} slice(f32[8,256]{1,0:T(8,128)} %get-tuple-element.19), slice={[0:1], [0:144]} | slice | bytes 1152 | tf_op jit(solution)/shard_map/slice | solution.py:387
Async XLA Ops:
  17.9 34.0 %copy-start = (bf16[18,8,512]{2,1,0:T(8,128)(2,1)S(1)}, bf16[18,8,512]{2,1,0:T(8,128)(2,1)}, u32[]{:S(2)}) copy-start(bf16[18,8,512]{2,1,0:T(8,128)(2,1)} %param.9) | copy-start | bytes 442372
  17.9 34.0 %copy-start.1 = (bf16[6,8,512]{2,1,0:T(8,128)(2,1)S(1)}, bf16[6,8,512]{2,1,0:T(8,128)(2,1)}, u32[]{:S(2)}) copy-start(bf16[6,8,512]{2,1,0:T(8,128)(2,1)} %param.10) | copy-start | bytes 147460
  17.9 34.0 %copy-start.2 = (bf16[2,8,512]{2,1,0:T(8,128)(2,1)S(1)}, bf16[2,8,512]{2,1,0:T(8,128)(2,1)}, u32[]{:S(2)}) copy-start(bf16[2,8,512]{2,1,0:T(8,128)(2,1)} %param.11) | copy-start | bytes 49156

commit v2 on v1

--- a/solution.py
+++ b/solution.py
@@ -18,7 +18,7 @@
 OVER = 217
 ROUNDS = -(-ALL // CAP)
 DAMPING = 0.5
-EXACT = lax.Precision.HIGHEST
+PIVOT = 8
 F32 = jnp.float32
 BF16 = jnp.bfloat16
 NT = (((1,), (1,)), ((), ()))
@@ -170,7 +170,7 @@
 
 
 def system_kernel(
-    blocks, m_ref, x_ref, out_ref, step_ref, wv, wp, zp, ap, gp, acc, acc_u, acc_g, turned, dm, st, woven
+    blocks, m_ref, count_ref, x_ref, out_ref, step_ref, wv, sv, iv, wp, zp, ap, gp, tiles, acc, acc_u, acc_g, turned, dm, st, woven
 ):
     m = m_ref[0]
     acc[...] = jnp.zeros_like(acc)
@@ -179,17 +179,44 @@
     gp[...] = jnp.zeros_like(gp)
     names = (iota((16, 128), 0) + 1).astype(F32).astype(BF16)
 
+    tiles[...] = jnp.zeros_like(tiles)
+    lane = iota((ROWS, 128), 1)
+
+    def append(s, used):
+        first = used // 128
+        shift = used % 128
+        two = [
+            pltpu.roll(x_ref[s, :, 0:128].astype(F32), shift, 1),
+            pltpu.roll(x_ref[s, :, 128:256].astype(F32), shift, 1),
+        ]
+        tiles[first] += jnp.where(lane >= shift, two[0], 0.0)
+        tiles[first + 1] += jnp.where(lane < shift, two[0], two[1])
+        tiles[first + 2] += jnp.where(lane < shift, two[1], 0.0)
+        return used + count_ref[s]
+
+    used = lax.fori_loop(0, blocks, append, jnp.int32(0))
+
     def spread(row):
         return jnp.broadcast_to(row, (16, 128)).astype(BF16)
 
-    def choose(slots, own, values):
-        out = jnp.zeros((16, 128), BF16)
+    def seats(slots, own):
+        number = jnp.zeros((16, 128), BF16)
         for o in range(OBS):
-            out = jnp.where(slots[o] == own, values[o], out)
-        return out
+            number = jnp.where(slots[o] == own, jnp.asarray(o + 1, BF16), number)
+        return number
+
+    def split(number):
+        index = jnp.maximum(number.astype(F32).astype(jnp.int32) - 1, 0)
+        return index[0:8, :], index[8:16, :]
+
+    def seated(value, index, has):
+        two = [jnp.take_along_axis(value, i, axis=0, mode="promise_in_bounds") for i in index]
+        return jnp.where(has, jnp.concatenate(two, axis=0).astype(BF16), jnp.zeros((16, 128), BF16))
 
     def chunk(s, carry):
-        slot, cam, res, w, z, g = block_values(x_ref[s].astype(F32))
+        slot, cam, res, w, z, g = block_values(
+            jnp.concatenate([tiles[2 * s], tiles[2 * s + 1]], axis=1)
+        )
         for a in range(9):
             for b in range(3):
                 wv[(a * 3 + b) * 8 : (a * 3 + b) * 8 + 8, :] = w[a, b]
@@ -206,9 +233,18 @@
         for h in range(2):
             lanes = slice(h * 128, h * 128 + 128)
             slots = [spread(slot[o : o + 1, lanes]) for o in range(OBS)]
+            for t in range(16):
+                number = seats(slots, names + jnp.asarray(16 * t, BF16))
+                low, high = split(number)
+                sv[t * 16 : t * 16 + 16, lanes] = number
+                iv[t * 16 : t * 16 + 8, lanes] = low
+                iv[t * 16 + 8 : t * 16 + 16, lanes] = high
+            number = seats(slots, mine)
+            index = split(number)
+            has = number > 0
 
             def own(value):
-                return choose(slots, mine, [spread(value[o : o + 1, lanes]) for o in range(OBS)])
+                return seated(value[:, lanes], index, has)
 
             for a in range(9):
                 for b in range(3):
@@ -226,31 +262,24 @@
         for a in range(9):
             for h in range(2):
                 lanes = slice(h * 128, h * 128 + 128)
-                slots = [spread(slot[o : o + 1, lanes]) for o in range(OBS)]
-                values = [
-                    [
-                        spread(wv[(a * 3 + b) * 8 + o : (a * 3 + b) * 8 + o + 1, lanes])
-                        for o in range(OBS)
-                    ]
-                    for b in range(3)
-                ]
+                values = [wv[(a * 3 + b) * 8 : (a * 3 + b) * 8 + 8, lanes] for b in range(3)]
                 for t in range(16):
-                    here = names + jnp.asarray(16 * t, BF16)
-                    outs = [jnp.zeros((16, 128), BF16)] * 3
-                    for o in range(OBS):
-                        same = slots[o] == here
-                        outs = [jnp.where(same, values[b][o], outs[b]) for b in range(3)]
+                    has = sv[t * 16 : t * 16 + 16, lanes] > 0
+                    index = (iv[t * 16 : t * 16 + 8, lanes], iv[t * 16 + 8 : t * 16 + 16, lanes])
                     for b in range(3):
                         wp[
                             a * CAMS + t * 16 : a * CAMS + t * 16 + 16,
                             b * CAP + h * 128 : b * CAP + h * 128 + 128,
-                        ] = outs[b]
-            acc[a] += lax.dot_general(
-                wp[a * CAMS : (a + 1) * CAMS, :], zp[...], NT, preferred_element_type=F32
-            )
+                        ] = seated(values[b], index, has)
+            if a % 3 == 2:
+                three = lax.dot_general(
+                    wp[(a - 2) * CAMS : (a + 1) * CAMS, :], zp[...], NT, preferred_element_type=F32
+                )
+                for q in range(3):
+                    acc[a - 2 + q] += three[q * CAMS : (q + 1) * CAMS, :]
         return carry
 
-    lax.fori_loop(0, blocks, chunk, 0)
+    lax.fori_loop(0, (used + CAP - 1) // CAP, chunk, 0)
 
     rows_u = iota((144, 144), 0)
     cols_u = iota((144, 144), 1)
@@ -274,7 +303,8 @@
         st[pl.ds(a, CAMS, stride=9), :] = jnp.concatenate(
             [acc[a, :, 128:144], jnp.zeros((CAMS, 112), F32)], axis=1
         )
-    for t in range(18):
+
+    def weave(t):
         lanes = slice(t * 128, t * 128 + 128)
         first = turned[lanes, :].T
         for a in range(8):
@@ -284,24 +314,56 @@
 
     whole = dm[...]
     flipped = whole.T
-    lane = iota((144, 256), 1)
-    mat = jnp.where(lane < 144, 0.5 * (whole[0:144, :] + flipped[0:144, :]), flipped[0:144, :])
-    sub = iota((144, 1), 0)
-    left, right = mat[:, 0:128], mat[:, 128:256]
-    for k in range(144):
-        if k < 128:
-            col = left[:, k : k + 1]
-        else:
-            col = right[:, k - 128 : k - 127]
-        scale = 1.0 / col[k : k + 1, :]
-        new_right = right[k : k + 1, :] * scale
-        less = col - (sub == k).astype(F32)
-        if k < 128:
-            left = left - less * (left[k : k + 1, :] * scale)
-        right = right - less * new_right
-    step = jnp.broadcast_to(-right[:, 16:17], (144, 128))
+    here = iota((8, 256), 1)
+    left, right = [], []
+    for i in range(18):
+        rows = slice(i * 8, i * 8 + 8)
+        tile = jnp.where(here < 144, 0.5 * (whole[rows, :] + flipped[rows, :]), flipped[rows, :])
+        left.append(tile[:, 0:128])
+        right.append(tile[:, 128:256])
+    sub = iota((8, 128), 0)
+    for k in range(0, 144, PIVOT):
+        top = k // 8
+        both = k < 128
+        cols = []
+        for q in range(PIVOT):
+            half, c = (left, k + q) if both else (right, k + q - 128)
+            cols.append([jnp.broadcast_to(half[i][:, c : c + 1], (8, 128)) for i in range(18)])
+
+        def row_of(tile, q):
+            r = (k + q) % 8
+            return jnp.broadcast_to(tile[r : r + 1, :], (8, 128))
+
+        piv = [[row_of(cols[j][top], q) for j in range(PIVOT)] for q in range(PIVOT)]
+        rhs = [
+            ([row_of(left[top], q)] if both else []) + [row_of(right[top], q)] for q in range(PIVOT)
+        ]
+        for q in range(PIVOT):
+            guess = pl.reciprocal(piv[q][q], approx=True)
+            for _ in range(2):
+                guess = guess * (2.0 - piv[q][q] * guess)
+            for j in range(q + 1, PIVOT):
+                piv[q][j] = piv[q][j] * guess
+            rhs[q] = [v * guess for v in rhs[q]]
+            for r in range(PIVOT):
+                if r != q:
+                    for j in range(q + 1, PIVOT):
+                        piv[r][j] = piv[r][j] - piv[r][q] * piv[q][j]
+                    rhs[r] = [v - piv[r][q] * n for v, n in zip(rhs[r], rhs[q])]
+        for i in range(18):
+            for q in range(PIVOT):
+                less = cols[q][i]
+                if i == top:
+                    less = less - (sub == (k + q) % 8).astype(F32)
+                if both:
+                    left[i] = left[i] - less * rhs[q][0]
+                right[i] = right[i] - less * rhs[q][-1]
+        if k % 8 == 0:
+            weave(k // 8)
+    for i in range(18):
+        woven[i * 8 : i * 8 + 8, :] = jnp.broadcast_to(-right[i][:, 16:17], (8, 128))
     for a in range(9):
-        st[pl.ds(a, 16, stride=9), :] = step[a * 16 : a * 16 + 16, :]
+        st[pl.ds(a, 16, stride=9), :] = woven[a * 16 : a * 16 + 16, :]
     step_ref[...] = st[0:256, :].T[0:8, :]
 
 
@@ -348,6 +410,7 @@
 
     def system(blocks):
         count = blocks.shape[0]
+        counts = blocks[:, COUNT, 0].astype(jnp.int32)
 
         def body(*refs):
             system_kernel(count, *refs)
@@ -358,14 +421,17 @@
                 jax.ShapeDtypeStruct((144, 9 * CAMS), F32),
                 jax.ShapeDtypeStruct((8, 256), F32),
             ),
-            in_specs=[pl.BlockSpec(memory_space=pltpu.SMEM), vmem],
+            in_specs=[pl.BlockSpec(memory_space=pltpu.SMEM)] * 2 + [vmem],
             out_specs=(vmem, vmem),
             scratch_shapes=[
                 pltpu.VMEM((216, CAP), F32),
+                pltpu.VMEM((CAMS, CAP), BF16),
+                pltpu.VMEM((CAMS, CAP), jnp.int32),
                 pltpu.VMEM((9 * CAMS, 3 * CAP), BF16),
                 pltpu.VMEM((144, 3 * CAP), BF16),
                 pltpu.VMEM((160, 2 * CAP), BF16),
                 pltpu.VMEM((16, 3 * CAP), BF16),
+                pltpu.VMEM((2 * count + 2, ROWS, 128), F32),
                 pltpu.VMEM((9, CAMS, 144), F32),
                 pltpu.VMEM((160, 144), F32),
                 pltpu.VMEM((16, 144), F32),
@@ -376,7 +442,7 @@
             ],
             compiler_params=params,
             name="system",
-        )(lax.axis_index("member").astype(jnp.int32).reshape(1), blocks)
+        )(lax.axis_index("member").astype(jnp.int32).reshape(1), counts, blocks)
 
     arrived = packed(0)
 

time: 119 us -> 86.4 us (0.73)
  Pallas kernels: 71.7 us -> 39.3 us
    pallas_call x1, Pallas kernels: 65.5 us -> 33 us  [system(): pl.pallas_call(body, out_shape=(jax.ShapeDtypeStruct((144, 9 * CAMS), F32...]
where the time goes in v2:
time: 86.4 us; the launch traced here: 87.1 us
  blocking collectives  43.7 us (51%)
  Pallas kernels  39.3 us (45%)
  other arithmetic  1.55 us (2%)
  between operations  1.32 us (2%)
  local copies, waits for them, and re-layouts  1.27 us (1%)
    pallas_call x1, Pallas kernels, system(): pl.pallas_call(body, out_shape=(jax.ShapeDtypeStruct((144, 9 * CAMS), F32...  33 us
    all_to_all x1, blocking collectives, packed(): lax.all_to_all(sent, 'member', split_axis=0, concat_axis=0, tiled=True)  32.7 us
    all_to_all x1, blocking collectives, per_device(): lax.all_to_all(far.reshape(8, 16, 256), 'cluster', split_axis=0, concat_a...  11 us
    pallas_call x1, Pallas kernels, packed(): pl.pallas_call(body, out_shape=jax.ShapeDtypeStruct((16, ROWS, CAP), BF16...  4.12 us
    pallas_call x1, Pallas kernels, per_device(): pl.pallas_call(sort_out_kernel, out_shape=(jax.ShapeDtypeStruct((16, PTS)...  2.19 us

profile of v2, /device:TPU:0, one launch (start us, length us, event | category | flops | bytes accessed | tf_op | source)
XLA Modules:
  0.0 87.1 jit_solution(12855029284137110219)
XLA Ops:
  0.6 2.2 %sort_out.1 = (bf16[16,512]{1,0:T(8,128)(2,1)S(1)}, bf16[128,256]{1,0:T(8,128)(2,1)}) custom-call(bf16[144,512]{1,0:T(8,128)(2,1)} %bitcast.12, bf16[48,512]{1,0:T(8,128)(2,1)} %bitcast.17, bf16[16,512]{1,0:T(8,128)(2,1)} %bitcast.20, s32[8,512]{1,0:T(8,128)} %oc_ref.1, s32[1,512]{1,0:T(1,128)} %bitcast.26, s32[16,128]{1,0:T(8,128)} %bitcast.24, ...), custom_call_target="tpu_custom_call" | custom-call | tf_op jit(solution)/shard_map/sort_out/pallas_call | solution.py:376
  2.8 11.0 %all_to_all.21 = bf16[8,16,256]{2,1,0:T(8,128)(2,1)S(1)} all-to-all(bf16[8,16,256]{2,1,0:T(8,128)(2,1)} %bitcast.23), channel_id=1, replica_groups=mesh['cluster'=8,'member'=16] {'cluster'}, dimensions={0} | all-to-all | bytes 131072 | tf_op jit(solution)/shard_map/all_to_all | solution.py:392
  13.8 4.1 %pack.5 = bf16[16,224,256]{2,1,0:T(8,128)(2,1)} custom-call(bf16[144,512]{1,0:T(8,128)(2,1)} %bitcast.13, bf16[48,512]{1,0:T(8,128)(2,1)} %bitcast.18, bf16[16,512]{1,0:T(8,128)(2,1)} %bitcast.21, bf16[16,512]{1,0:T(8,128)(2,1)S(1)} %get-tuple-element.32.refs_3_, bf16[128,256]{1,0:T(8,128)(2,1)S(1)} %bitcast.15), custom_call_target="tpu_custom_call" | custom-call | tf_op jit(solution)/shard_map/pack/pallas_call | solution.py:400
  18.0 0.0 copy-start
  18.0 0.0 copy-start.1
  18.0 0.0 copy-start.2
  18.0 32.7 %all_to_all.22 = bf16[16,224,256]{2,1,0:T(8,128)(2,1)S(1)} all-to-all(bf16[16,224,256]{2,1,0:T(8,128)(2,1)} %pack.5), channel_id=1, replica_groups=mesh['cluster'=8,'member'=16] {'member'}, dimensions={0} | all-to-all | bytes 3670016 | tf_op jit(solution)/shard_map/all_to_all | solution.py:409
  50.6 0.6 slice_reduce_fusion
  51.9 0.0 copy-done
  51.9 0.0 copy-done.1
  51.9 0.0 copy-done.2
  52.0 35.2 %conditional.1 = (f32[144,2304]{1,0:T(8,128)}, f32[144]{0:T(256)}) conditional(s32[]{:T(128)} %convert_element_type.13, bf16[16,224,256]{2,1,0:T(8,128)(2,1)S(1)} %all_to_all.22, (bf16[144,512]{1,0:T(8,128)(2,1)S(1)}, bf16[48,512]{1,0:T(8,128)(2,1)S(1)}, bf16[16,512]{1,0:T(8,128)(2,1)S(1)}, bf16[16,512]{1,0:T(8,128)(2,1)S(1)}, ...), branch_computations={%region_1.0_spmd, %region_2.0_spmd} | conditional | flops 50 | bytes 22021636 | solution.py:452
  52.0 0.9 %convert_reduce_fusion.refs_1_ = s32[16]{0:T(128)} fusion(bf16[16,224,256]{2,1,0:T(8,128)(2,1)S(1)} %refs_2_), kind=kLoop, calls=%fused_computation | loop fusion | flops 16 | bytes 96 | tf_op jit(solution)/shard_map/cond/branch_0_fun/convert_element_type | solution.py:413
  52.9 33.0 %system.2 = (f32[144,2304]{1,0:T(8,128)}, f32[8,256]{1,0:T(8,128)}) custom-call(s32[1]{0:T(128)} %bitcast.refs_0_, s32[16]{0:T(128)} %convert_reduce_fusion.refs_1_, bf16[16,224,256]{2,1,0:T(8,128)(2,1)S(1)} %refs_2_), custom_call_target="tpu_custom_call" | custom-call | tf_op jit(solution)/shard_map/cond/branch_0_fun/system/pallas_call | solution.py:418
  85.9 1.3 %slice.12 = f32[1,144]{1,0:T(1,128)} slice(f32[8,256]{1,0:T(8,128)} %get-tuple-element.19), slice={[0:1], [0:144]} | slice | bytes 1152 | tf_op jit(solution)/shard_map/slice | solution.py:453
Async XLA Ops:
  18.0 34.0 %copy-start = (bf16[18,8,512]{2,1,0:T(8,128)(2,1)S(1)}, bf16[18,8,512]{2,1,0:T(8,128)(2,1)}, u32[]{:S(2)}) copy-start(bf16[18,8,512]{2,1,0:T(8,128)(2,1)} %param.9) | copy-start | bytes 442372
  18.0 34.0 %copy-start.1 = (bf16[6,8,512]{2,1,0:T(8,128)(2,1)S(1)}, bf16[6,8,512]{2,1,0:T(8,128)(2,1)}, u32[]{:S(2)}) copy-start(bf16[6,8,512]{2,1,0:T(8,128)(2,1)} %param.10) | copy-start | bytes 147460
  18.0 34.0 %copy-start.2 = (bf16[2,8,512]{2,1,0:T(8,128)(2,1)S(1)}, bf16[2,8,512]{2,1,0:T(8,128)(2,1)}, u32[]{:S(2)}) copy-start(bf16[2,8,512]{2,1,0:T(8,128)(2,1)} %param.11) | copy-start | bytes 49156

commit v3 on v2

--- a/solution.py
+++ b/solution.py
@@ -21,6 +21,13 @@
 PIVOT = 8
 F32 = jnp.float32
 BF16 = jnp.bfloat16
+ALONG_ROWS = lax.GatherDimensionNumbers(
+    offset_dims=(),
+    collapsed_slice_dims=(0,),
+    start_index_map=(0,),
+    operand_batching_dims=(1,),
+    start_indices_batching_dims=(1,),
+)
 NT = (((1,), (1,)), ((), ()))
 VMEM_BYTES = 56 * 1024 * 1024
 
@@ -106,11 +113,13 @@
     rank = count - 1.0 - first_rank
     rank = jnp.where(touch & (rank >= 0.0) & (rank < CAP), rank, -1.0)
     over = jnp.max((total > CAP).astype(F32), axis=0, keepdims=True)
-    seat = iota((CAP, ALL), 0).astype(F32)
+    seat = iota((CAP, ALL), 0).astype(F32).astype(BF16)
     here = jnp.clip(total - first_rank, 0.0, float(CAP))
     line = iota((16, CAP), 0)
     for d in range(16):
-        chosen = (jnp.broadcast_to(rank[d : d + 1, :], (CAP, ALL)) == seat).astype(BF16)
+        asked = jnp.broadcast_to(rank[d : d + 1, :], (16, ALL)).astype(BF16)
+        asked = jnp.concatenate([asked] * (CAP // 16), axis=0)
+        chosen = jnp.where(asked == seat, jnp.asarray(1, BF16), jnp.asarray(0, BF16))
         moved = lax.dot_general(feat[...], chosen, NT, preferred_element_type=F32)
         out_ref[d, 0:208, :] = moved[0:208, :].astype(BF16)
         tail = jnp.where(
@@ -170,7 +179,7 @@
 
 
 def system_kernel(
-    blocks, m_ref, count_ref, x_ref, out_ref, step_ref, wv, sv, iv, wp, zp, ap, gp, tiles, acc, acc_u, acc_g, turned, dm, st, woven
+    blocks, m_ref, x_ref, out_ref, step_ref, wv, iv, wp, zp, ap, gp, tiles, acc, acc_u, acc_g, turned, dm, st, woven, counts
 ):
     m = m_ref[0]
     acc[...] = jnp.zeros_like(acc)
@@ -179,8 +188,11 @@
     gp[...] = jnp.zeros_like(gp)
     names = (iota((16, 128), 0) + 1).astype(F32).astype(BF16)
 
-    tiles[...] = jnp.zeros_like(tiles)
     lane = iota((ROWS, 128), 1)
+    place = (iota((16, 128), 0) == COUNT - SLOT) & (iota((16, 128), 1) == 0)
+    for s in range(blocks):
+        line = x_ref[s, SLOT:ROWS, 0:128].astype(F32)
+        counts[s] = jnp.sum(jnp.where(place, line, 0.0)).astype(jnp.int32)
 
     def append(s, used):
         first = used // 128
@@ -189,29 +201,31 @@
             pltpu.roll(x_ref[s, :, 0:128].astype(F32), shift, 1),
             pltpu.roll(x_ref[s, :, 128:256].astype(F32), shift, 1),
         ]
-        tiles[first] += jnp.where(lane >= shift, two[0], 0.0)
-        tiles[first + 1] += jnp.where(lane < shift, two[0], two[1])
-        tiles[first + 2] += jnp.where(lane < shift, two[1], 0.0)
-        return used + count_ref[s]
-
+        tiles[first] = jnp.where(lane >= shift, two[0], tiles[first])
+        tiles[first + 1] = jnp.where(lane < shift, two[0], two[1])
+        tiles[first + 2] = jnp.where(lane < shift, two[1], 0.0)
+        return used + counts[s]
+
+    tiles[0] = jnp.zeros((ROWS, 128), F32)
     used = lax.fori_loop(0, blocks, append, jnp.int32(0))
+    tiles[used // 128 + 1] = jnp.zeros((ROWS, 128), F32)
 
     def spread(row):
         return jnp.broadcast_to(row, (16, 128)).astype(BF16)
 
     def seats(slots, own):
-        number = jnp.zeros((16, 128), BF16)
+        number = jnp.full((16, 128), 8, jnp.int16)
         for o in range(OBS):
-            number = jnp.where(slots[o] == own, jnp.asarray(o + 1, BF16), number)
+            number = jnp.where(slots[o] == own, jnp.int16(o), number)
         return number
 
-    def split(number):
-        index = jnp.maximum(number.astype(F32).astype(jnp.int32) - 1, 0)
-        return index[0:8, :], index[8:16, :]
-
-    def seated(value, index, has):
-        two = [jnp.take_along_axis(value, i, axis=0, mode="promise_in_bounds") for i in index]
-        return jnp.where(has, jnp.concatenate(two, axis=0).astype(BF16), jnp.zeros((16, 128), BF16))
+    def table(value):
+        return jnp.concatenate([value, jnp.zeros_like(value)], axis=0).astype(BF16)
+
+    def seated(values, index):
+        return lax.gather(
+            values, index[..., None], ALONG_ROWS, (1, 1), mode=lax.GatherScatterMode.PROMISE_IN_BOUNDS
+        )
 
     def chunk(s, carry):
         slot, cam, res, w, z, g = block_values(
@@ -219,7 +233,7 @@
         )
         for a in range(9):
             for b in range(3):
-                wv[(a * 3 + b) * 8 : (a * 3 + b) * 8 + 8, :] = w[a, b]
+                wv[(a * 3 + b) * 16 : (a * 3 + b) * 16 + 16, :] = table(w[a, b])
         for b in range(3):
             high = g[b].astype(BF16)
             rest = g[b] - high.astype(F32)
@@ -234,17 +248,11 @@
             lanes = slice(h * 128, h * 128 + 128)
             slots = [spread(slot[o : o + 1, lanes]) for o in range(OBS)]
             for t in range(16):
-                number = seats(slots, names + jnp.asarray(16 * t, BF16))
-                low, high = split(number)
-                sv[t * 16 : t * 16 + 16, lanes] = number
-                iv[t * 16 : t * 16 + 8, lanes] = low
-                iv[t * 16 + 8 : t * 16 + 16, lanes] = high
-            number = seats(slots, mine)
-            index = split(number)
-            has = number > 0
+                iv[t * 16 : t * 16 + 16, lanes] = seats(slots, names + jnp.asarray(16 * t, BF16))
+            index = seats(slots, mine)
 
             def own(value):
-                return seated(value[:, lanes], index, has)
+                return seated(table(value[:, lanes]), index)
 
             for a in range(9):
                 for b in range(3):
@@ -262,15 +270,14 @@
         for a in range(9):
             for h in range(2):
                 lanes = slice(h * 128, h * 128 + 128)
-                values = [wv[(a * 3 + b) * 8 : (a * 3 + b) * 8 + 8, lanes] for b in range(3)]
+                values = [wv[(a * 3 + b) * 16 : (a * 3 + b) * 16 + 16, lanes] for b in range(3)]
                 for t in range(16):
-                    has = sv[t * 16 : t * 16 + 16, lanes] > 0
-                    index = (iv[t * 16 : t * 16 + 8, lanes], iv[t * 16 + 8 : t * 16 + 16, lanes])
+                    index = iv[t * 16 : t * 16 + 16, lanes]
                     for b in range(3):
                         wp[
                             a * CAMS + t * 16 : a * CAMS + t * 16 + 16,
                             b * CAP + h * 128 : b * CAP + h * 128 + 128,
-                        ] = seated(values[b], index, has)
+                        ] = seated(values[b], index)
             if a % 3 == 2:
                 three = lax.dot_general(
                     wp[(a - 2) * CAMS : (a + 1) * CAMS, :], zp[...], NT, preferred_element_type=F32
@@ -338,18 +345,29 @@
         rhs = [
             ([row_of(left[top], q)] if both else []) + [row_of(right[top], q)] for q in range(PIVOT)
         ]
-        for q in range(PIVOT):
-            guess = pl.reciprocal(piv[q][q], approx=True)
+        for q in range(0, PIVOT, 2):
+            a, b, c, d = piv[q][q], piv[q][q + 1], piv[q + 1][q], piv[q + 1][q + 1]
+            det = a * d - b * c
+            guess = pl.reciprocal(det, approx=True)
             for _ in range(2):
-                guess = guess * (2.0 - piv[q][q] * guess)
-            for j in range(q + 1, PIVOT):
-                piv[q][j] = piv[q][j] * guess
-            rhs[q] = [v * guess for v in rhs[q]]
+                guess = guess * (2.0 - det * guess)
+            ia, ib, ic, id_ = d * guess, b * guess, c * guess, a * guess
+            top_two = [piv[q][q + 2 :] + rhs[q], piv[q + 1][q + 2 :] + rhs[q + 1]]
+            new = [
+                [ia * u - ib * v for u, v in zip(*top_two)],
+                [id_ * v - ic * u for u, v in zip(*top_two)],
+            ]
+            left_over = PIVOT - q - 2
             for r in range(PIVOT):
-                if r != q:
-                    for j in range(q + 1, PIVOT):
-                        piv[r][j] = piv[r][j] - piv[r][q] * piv[q][j]
-                    rhs[r] = [v - piv[r][q] * n for v, n in zip(rhs[r], rhs[q])]
+                if r in (q, q + 1):
+                    rest = new[r - q]
+                else:
+                    rest = [
+                        w - piv[r][q] * u - piv[r][q + 1] * v
+                        for w, u, v in zip(piv[r][q + 2 :] + rhs[r], *new)
+                    ]
+                piv[r] = piv[r][: q + 2] + rest[:left_over]
+                rhs[r] = rest[left_over:]
         for i in range(18):
             for q in range(PIVOT):
                 less = cols[q][i]
@@ -364,7 +382,7 @@
         woven[i * 8 : i * 8 + 8, :] = jnp.broadcast_to(-right[i][:, 16:17], (8, 128))
     for a in range(9):
         st[pl.ds(a, 16, stride=9), :] = woven[a * 16 : a * 16 + 16, :]
-    step_ref[...] = st[0:256, :].T[0:8, :]
+    step_ref[...] = st[0:256, :].T[0, 0:144]
 
 
 def per_device(cam_jac, point_jac, residuals, obs_camera, obs_count, new_cluster, new_slot):
@@ -410,7 +428,6 @@
 
     def system(blocks):
         count = blocks.shape[0]
-        counts = blocks[:, COUNT, 0].astype(jnp.int32)
 
         def body(*refs):
             system_kernel(count, *refs)
@@ -419,14 +436,13 @@
             body,
             out_shape=(
                 jax.ShapeDtypeStruct((144, 9 * CAMS), F32),
-                jax.ShapeDtypeStruct((8, 256), F32),
+                jax.ShapeDtypeStruct((144,), F32),
             ),
-            in_specs=[pl.BlockSpec(memory_space=pltpu.SMEM)] * 2 + [vmem],
+            in_specs=[pl.BlockSpec(memory_space=pltpu.SMEM), vmem],
             out_specs=(vmem, vmem),
             scratch_shapes=[
-                pltpu.VMEM((216, CAP), F32),
-                pltpu.VMEM((CAMS, CAP), BF16),
-                pltpu.VMEM((CAMS, CAP), jnp.int32),
+                pltpu.VMEM((432, CAP), BF16),
+                pltpu.VMEM((CAMS, CAP), jnp.int16),
                 pltpu.VMEM((9 * CAMS, 3 * CAP), BF16),
                 pltpu.VMEM((144, 3 * CAP), BF16),
                 pltpu.VMEM((160, 2 * CAP), BF16),
@@ -439,10 +455,11 @@
                 pltpu.VMEM((256, 256), F32),
                 pltpu.VMEM((9 * CAMS, 128), F32),
                 pltpu.VMEM((18 * 144, 128), F32),
+                pltpu.SMEM((count,), jnp.int32),
             ],
             compiler_params=params,
             name="system",
-        )(lax.axis_index("member").astype(jnp.int32).reshape(1), counts, blocks)
+        )(lax.axis_index("member").astype(jnp.int32).reshape(1), blocks)
 
     arrived = packed(0)
 
@@ -450,7 +467,7 @@
         return system(jnp.concatenate([arrived] + [packed(t) for t in range(1, ROUNDS)], axis=0))
 
     matrix, step = lax.cond(jnp.max(arrived[:, OVER, 0]) > 0, more_rounds, system, arrived)
-    return matrix, step[0, 0:144]
+    return matrix, step
 
 
 def solution(mesh):

time: 86.4 us -> 78.9 us (0.913)
  Pallas kernels: 39.3 us -> 34.1 us
  local copies, waits for them, and re-layouts: 1.27 us -> 0.01 us
  other arithmetic: 1.55 us -> 0.62 us
    pallas_call x1, Pallas kernels: 33 us -> 27.8 us  [system(): pl.pallas_call(body, out_shape=(jax.ShapeDtypeStruct((144, 9 * CAMS), F32...]
    slice x1 -> x0, local copies, waits for them, and re-layouts: 1.26 us -> none  [per_device(): return (matrix, step[0, 0:144])]
    convert_element_type x1 -> x0, other arithmetic: 0.93 us -> none  [system(): counts = blocks[:, COUNT, 0].astype(jnp.int32)]
where the time goes in v3:
time: 78.9 us; the launch traced here: 79.8 us
  blocking collectives  43.7 us (55%)
  Pallas kernels  34.1 us (43%)
  between operations  1.32 us (2%)
    all_to_all x1, blocking collectives, packed(): lax.all_to_all(sent, 'member', split_axis=0, concat_axis=0, tiled=True)  32.7 us
    pallas_call x1, Pallas kernels, system(): pl.pallas_call(body, out_shape=(jax.ShapeDtypeStruct((144, 9 * CAMS), F32...  27.8 us
    all_to_all x1, blocking collectives, per_device(): lax.all_to_all(far.reshape(8, 16, 256), 'cluster', split_axis=0, concat_a...  11 us
    pallas_call x1, Pallas kernels, packed(): pl.pallas_call(body, out_shape=jax.ShapeDtypeStruct((16, ROWS, CAP), BF16...  4.14 us
    pallas_call x1, Pallas kernels, per_device(): pl.pallas_call(sort_out_kernel, out_shape=(jax.ShapeDtypeStruct((16, PTS)...  2.19 us

profile of v3, /device:TPU:0, one launch (start us, length us, event | category | flops | bytes accessed | tf_op | source)
XLA Modules:
  0.0 79.8 jit_solution(16135785612408833924)
XLA Ops:
  0.6 2.2 %sort_out.1 = (bf16[16,512]{1,0:T(8,128)(2,1)S(1)}, bf16[128,256]{1,0:T(8,128)(2,1)}) custom-call(bf16[144,512]{1,0:T(8,128)(2,1)} %bitcast.10, bf16[48,512]{1,0:T(8,128)(2,1)} %bitcast.15, bf16[16,512]{1,0:T(8,128)(2,1)} %bitcast.18, s32[8,512]{1,0:T(8,128)} %oc_ref.1, s32[1,512]{1,0:T(1,128)} %bitcast.24, s32[16,128]{1,0:T(8,128)} %bitcast.22, ...), custom_call_target="tpu_custom_call" | custom-call | tf_op jit(solution)/shard_map/sort_out/pallas_call | solution.py:394
  2.8 11.0 %all_to_all.21 = bf16[8,16,256]{2,1,0:T(8,128)(2,1)S(1)} all-to-all(bf16[8,16,256]{2,1,0:T(8,128)(2,1)} %bitcast.21), channel_id=1, replica_groups=mesh['cluster'=8,'member'=16] {'cluster'}, dimensions={0} | all-to-all | bytes 131072 | tf_op jit(solution)/shard_map/all_to_all | solution.py:410
  13.8 4.1 %pack.5 = bf16[16,224,256]{2,1,0:T(8,128)(2,1)} custom-call(bf16[144,512]{1,0:T(8,128)(2,1)} %bitcast.11, bf16[48,512]{1,0:T(8,128)(2,1)} %bitcast.16, bf16[16,512]{1,0:T(8,128)(2,1)} %bitcast.19, bf16[16,512]{1,0:T(8,128)(2,1)S(1)} %get-tuple-element.23.refs_3_, bf16[128,256]{1,0:T(8,128)(2,1)S(1)} %bitcast.13), custom_call_target="tpu_custom_call" | custom-call | tf_op jit(solution)/shard_map/pack/pallas_call | solution.py:418
  18.0 0.0 copy-start
  18.0 0.0 copy-start.1
  18.0 0.0 copy-start.2
  18.0 32.7 %all_to_all.22 = bf16[16,224,256]{2,1,0:T(8,128)(2,1)S(1)} all-to-all(bf16[16,224,256]{2,1,0:T(8,128)(2,1)} %pack.5), channel_id=1, replica_groups=mesh['cluster'=8,'member'=16] {'member'}, dimensions={0} | all-to-all | bytes 3670016 | tf_op jit(solution)/shard_map/all_to_all | solution.py:427
  50.7 0.6 slice_reduce_fusion
  51.9 0.0 copy-done
  52.0 0.0 copy-done.1
  52.0 0.0 copy-done.2
  52.0 27.8 %conditional.1 = ((f32[144,2304]{1,0:T(8,128)}, f32[144]{0:T(256)})) conditional(s32[]{:T(128)} %convert_element_type.3, bf16[16,224,256]{2,1,0:T(8,128)(2,1)S(1)} %all_to_all.22, (bf16[144,512]{1,0:T(8,128)(2,1)S(1)}, bf16[48,512]{1,0:T(8,128)(2,1)S(1)}, bf16[16,512]{1,0:T(8,128)(2,1)S(1)}, bf16[16,512]{1,0:T(8,128)(2,1)S(1)}, ...), branch_computations={%region_1.0_spmd, %region_2.0_spmd} | conditional | flops 5505026 | bytes 22020188 | solution.py:469
  52.0 27.8 %system.2 = (f32[144,2304]{1,0:T(8,128)}, f32[144]{0:T(256)}) custom-call(s32[1]{0:T(128)} %bitcast.refs_0_, bf16[16,224,256]{2,1,0:T(8,128)(2,1)S(1)} %refs_1_), custom_call_target="tpu_custom_call" | custom-call | tf_op jit(solution)/shard_map/cond/branch_0_fun/system/pallas_call | solution.py:435
Async XLA Ops:
  18.0 34.0 %copy-start = (bf16[18,8,512]{2,1,0:T(8,128)(2,1)S(1)}, bf16[18,8,512]{2,1,0:T(8,128)(2,1)}, u32[]{:S(2)}) copy-start(bf16[18,8,512]{2,1,0:T(8,128)(2,1)} %param.9) | copy-start | bytes 442372
  18.0 34.0 %copy-start.1 = (bf16[6,8,512]{2,1,0:T(8,128)(2,1)S(1)}, bf16[6,8,512]{2,1,0:T(8,128)(2,1)}, u32[]{:S(2)}) copy-start(bf16[6,8,512]{2,1,0:T(8,128)(2,1)} %param.10) | copy-start | bytes 147460
  18.0 34.0 %copy-start.2 = (bf16[2,8,512]{2,1,0:T(8,128)(2,1)S(1)}, bf16[2,8,512]{2,1,0:T(8,128)(2,1)}, u32[]{:S(2)}) copy-start(bf16[2,8,512]{2,1,0:T(8,128)(2,1)} %param.11) | copy-start | bytes 49156

commit v4 on v3

--- a/solution.py
+++ b/solution.py
@@ -19,6 +19,7 @@
 ROUNDS = -(-ALL // CAP)
 DAMPING = 0.5
 PIVOT = 8
+STEP = 16
 F32 = jnp.float32
 BF16 = jnp.bfloat16
 ALONG_ROWS = lax.GatherDimensionNumbers(
@@ -128,6 +129,66 @@
             jnp.where(line == 8, here[d : d + 1, :], jnp.where(line == 9, over, 0.0)),
         )
         out_ref[d, 208:224, :] = tail.astype(BF16)
+
+
+def touched(slots):
+    owner = ((slots.astype(jnp.int32) + 15) >> 4) - 1
+    member = iota((16, slots.shape[1]), 0)
+    touch = jnp.zeros(member.shape, jnp.bool_)
+    for o in range(OBS):
+        touch = touch | (jnp.broadcast_to(owner[o : o + 1, :], member.shape) == member)
+    return touch.astype(F32)
+
+
+def move(features, rank):
+    points = rank.shape[1]
+    seat = iota((CAP, points), 0).astype(F32).astype(BF16)
+    asked = jnp.broadcast_to(rank, (16, points)).astype(BF16)
+    asked = jnp.concatenate([asked] * (CAP // 16), axis=0)
+    chosen = jnp.where(asked == seat, jnp.asarray(1, BF16), jnp.asarray(0, BF16))
+    return lax.dot_general(features, chosen, NT, preferred_element_type=F32)
+
+
+def pack_home_kernel(cam_ref, pt_ref, res_ref, slot_ref, out_ref, total_ref, feat):
+    feat[0:144, :] = cam_ref[...]
+    feat[144:192, :] = pt_ref[...]
+    feat[192:208, :] = res_ref[...]
+    feat[208:224, :] = slot_ref[...]
+    hits = touched(slot_ref[...].astype(F32)[0:8, :])
+    count = running_count(hits)
+    rank = jnp.where((hits > 0.0) & (count <= CAP), count - 1.0, -1.0)
+    total_ref[...] = jnp.broadcast_to(jnp.max(count, axis=1, keepdims=True), (16, 128))
+    for d in range(16):
+        out_ref[d] = move(feat[...], rank[d : d + 1, :]).astype(BF16)
+
+
+def pack_arrived_kernel(home_ref, total_ref, far_ref, out_ref, feat, ranks, marks):
+    step = pl.program_id(0)
+
+    @pl.when(step == 0)
+    def _():
+        feat[...] = far_ref[...].astype(F32).T[0:ROWS, :].astype(BF16)
+        hits = touched(feat[208:224, :].astype(F32)[0:8, :])
+        count = running_count(hits) + total_ref[...]
+        total = jnp.max(count, axis=1, keepdims=True)
+        ranks[...] = jnp.where((hits > 0.0) & (count <= CAP), count - 1.0, -1.0)
+        over = jnp.max((total > CAP).astype(F32), axis=0, keepdims=True)
+        marks[0:16, :] = jnp.broadcast_to(jnp.minimum(total, float(CAP)), (16, CAP))
+        marks[16:24, :] = jnp.broadcast_to(over, (8, CAP))
+
+    line = iota((16, CAP), 0)
+    for i in range(STEP):
+        d = step * STEP + i
+        moved = move(feat[...], ranks[pl.ds(d, 1), :])
+        out_ref[i, 0:208, :] = home_ref[i, 0:208, :] + moved[0:208, :].astype(BF16)
+        tail = jnp.where(
+            line < 8,
+            home_ref[i, 208:224, :].astype(F32) + moved[208:224, :],
+            jnp.where(
+                line == 8, marks[pl.ds(d, 1), :], jnp.where(line == 9, marks[16:17, :], 0.0)
+            ),
+        )
+        out_ref[i, 208:224, :] = tail.astype(BF16)
 
 
 def block_values(f):
@@ -411,6 +472,38 @@
         far.reshape(8, 16, 256), "cluster", split_axis=0, concat_axis=0, tiled=True
     ).reshape(FAR, 256)
 
+    home, home_total = pl.pallas_call(
+        pack_home_kernel,
+        out_shape=(
+            jax.ShapeDtypeStruct((16, ROWS, CAP), BF16),
+            jax.ShapeDtypeStruct((16, 128), F32),
+        ),
+        in_specs=[vmem] * 4,
+        out_specs=(vmem, vmem),
+        scratch_shapes=[pltpu.VMEM((ROWS, PTS), BF16)],
+        compiler_params=params,
+        cost_estimate=pl.CostEstimate(flops=2 * 16 * ROWS * PTS * CAP, bytes_accessed=2**21, transcendentals=0),
+        name="pack_home",
+    )(cam, pt, res, slots)
+    first = pl.pallas_call(
+        pack_arrived_kernel,
+        out_shape=jax.ShapeDtypeStruct((16, ROWS, CAP), BF16),
+        grid=(16 // STEP,),
+        in_specs=[
+            pl.BlockSpec((STEP, ROWS, CAP), lambda g: (g, 0, 0)),
+            pl.BlockSpec((16, 128), lambda g: (0, 0)),
+            pl.BlockSpec((FAR, 256), lambda g: (0, 0)),
+        ],
+        out_specs=pl.BlockSpec((STEP, ROWS, CAP), lambda g: (g, 0, 0)),
+        scratch_shapes=[
+            pltpu.VMEM((ROWS, FAR), BF16),
+            pltpu.VMEM((16, 128), F32),
+            pltpu.VMEM((24, CAP), F32),
+        ],
+        compiler_params=params,
+        name="pack_arrived",
+    )(home, home_total, far)
+
     def packed(turn):
         def body(*refs):
             pack_kernel(float(turn * CAP), *refs)
@@ -461,7 +554,7 @@
             name="system",
         )(lax.axis_index("member").astype(jnp.int32).reshape(1), blocks)
 
-    arrived = packed(0)
+    arrived = lax.all_to_all(first, "member", split_axis=0, concat_axis=0, tiled=True)
 
     def more_rounds(arrived):
         return system(jnp.concatenate([arrived] + [packed(t) for t in range(1, ROUNDS)], axis=0))

time: 78.9 us -> 78.4 us (level)
  blocking collectives: 43.7 us -> 32.7 us
  starting transfers between devices: 0 us -> 5.4 us
  Pallas kernels: 34.1 us -> 37.4 us
  waiting for transfers between devices: 0 us -> 1.82 us
    all_to_all x2 -> x1, blocking collectives: 43.7 us -> 32.7 us  [per_device(): lax.all_to_all(first, 'member', split_axis=0, concat_axis=0, tiled=True)]
    all_to_all x0 -> x1, starting transfers between devices: none -> 5.4 us  [per_device(): lax.all_to_all(far.reshape(8, 16, 256), 'cluster', split_axis=0, concat_a...]
    pallas_call x1 -> x2, Pallas kernels: 4.14 us -> 7.45 us  [the longest x1 3.8 us: per_device(): pl.pallas_call(pack_home_kernel, out_shape=(jax.ShapeDtypeStruct((16, ROW...]
    all_to_all x0 -> x1, waiting for transfers between devices: none -> 1.82 us  [per_device(): lax.all_to_all(far.reshape(8, 16, 256), 'cluster', split_axis=0, concat_a...]
  transfers between devices with their start and end apart: 0 -> 1, of which waited for: 0 -> 1; matrix products, arithmetic and copies ran while one was open for 0% -> 0% of each run, Pallas kernels for 0% -> 5%
where the time goes in v4:
time: 78.4 us; the launch traced here: 79.3 us
  Pallas kernels  37.4 us (48%)
  blocking collectives  32.7 us (42%)
  starting transfers between devices  5.4 us (7%)
  waiting for transfers between devices  1.82 us (2%)
  between operations  1.32 us (2%)
    all_to_all x1, blocking collectives, per_device(): lax.all_to_all(first, 'member', split_axis=0, concat_axis=0, tiled=True)  32.7 us
    pallas_call x1, Pallas kernels, system(): pl.pallas_call(body, out_shape=(jax.ShapeDtypeStruct((144, 9 * CAMS), F32...  27.8 us
    all_to_all x1, starting transfers between devices, per_device(): lax.all_to_all(far.reshape(8, 16, 256), 'cluster', split_axis=0, concat_a...  5.4 us
    pallas_call x1, Pallas kernels, per_device(): pl.pallas_call(pack_home_kernel, out_shape=(jax.ShapeDtypeStruct((16, ROW...  3.8 us
    pallas_call x1, Pallas kernels, per_device(): pl.pallas_call(pack_arrived_kernel, out_shape=jax.ShapeDtypeStruct((16, R...  3.64 us
    pallas_call x1, Pallas kernels, per_device(): pl.pallas_call(sort_out_kernel, out_shape=(jax.ShapeDtypeStruct((16, PTS)...  2.19 us
    all_to_all x1, waiting for transfers between devices, per_device(): lax.all_to_all(far.reshape(8, 16, 256), 'cluster', split_axis=0, concat_a...  1.82 us
  transfers between devices with their start and end apart: 1, of which 1 were waited for; matrix products, arithmetic and copies ran while one was open for 0% of the time, Pallas kernels for 5%

profile of v4, /device:TPU:0, one launch (start us, length us, event | category | flops | bytes accessed | tf_op | source)
XLA Modules:
  0.0 79.3 jit_solution(3263489243239180861)
XLA Ops:
  0.6 2.2 %sort_out.1 = (bf16[16,512]{1,0:T(8,128)(2,1)S(1)}, bf16[128,256]{1,0:T(8,128)(2,1)}) custom-call(bf16[144,512]{1,0:T(8,128)(2,1)} %bitcast.10, bf16[48,512]{1,0:T(8,128)(2,1)} %bitcast.15, bf16[16,512]{1,0:T(8,128)(2,1)} %bitcast.18, s32[8,512]{1,0:T(8,128)} %oc_ref.1, s32[1,512]{1,0:T(1,128)} %bitcast.24, s32[16,128]{1,0:T(8,128)} %bitcast.22, ...), custom_call_target="tpu_custom_call" | custom-call | tf_op jit(solution)/shard_map/sort_out/pallas_call | solution.py:455
  2.8 5.4 %all-to-all-start.2 = ((bf16[8,16,256]{2,1,0:T(8,128)(2,1)}), bf16[8,16,256]{2,1,0:T(8,128)(2,1)S(1)}, u32[]{:S(2)}, u32[]{:S(2)}) async-start(bf16[8,16,256]{2,1,0:T(8,128)(2,1)} %bitcast.21), calls=%async_computation.2 | async-start | bytes 131072 | tf_op jit(solution)/shard_map/all_to_all | solution.py:471
  8.2 3.8 %pack_home.1 = (bf16[16,224,256]{2,1,0:T(8,128)(2,1)}, f32[16,128]{1,0:T(8,128)}) custom-call(bf16[144,512]{1,0:T(8,128)(2,1)} %bitcast.11, bf16[48,512]{1,0:T(8,128)(2,1)} %bitcast.16, bf16[16,512]{1,0:T(8,128)(2,1)} %bitcast.19, bf16[16,512]{1,0:T(8,128)(2,1)S(1)} %get-tuple-element.25.slot_ref), custom_call_target="tpu_custom_call" | custom-call | flops 939524096 | bytes 2097152 | tf_op jit(solution)/shard_map/pack_home/pallas_call | solution.py:475
  12.0 1.8 %all-to-all-done.2 = bf16[8,16,256]{2,1,0:T(8,128)(2,1)S(1)} async-done(((bf16[8,16,256]{2,1,0:T(8,128)(2,1)}), bf16[8,16,256]{2,1,0:T(8,128)(2,1)S(1)}, u32[]{:S(2)}, u32[]{:S(2)}) %all-to-all-start.2) | async-done | bytes 65568 | tf_op jit(solution)/shard_map/all_to_all | solution.py:471
  13.8 3.6 %pack_arrived.1 = bf16[16,224,256]{2,1,0:T(8,128)(2,1)} custom-call(bf16[16,224,256]{2,1,0:T(8,128)(2,1)} %get-tuple-element.26.home_ref, f32[16,128]{1,0:T(8,128)} %get-tuple-element.27.total_ref, bf16[128,256]{1,0:T(8,128)(2,1)S(1)} %bitcast.13), custom_call_target="tpu_custom_call" | custom-call | tf_op jit(solution)/shard_map/pack_arrived/pallas_call | solution.py:488
  17.5 0.0 copy-start
  17.5 0.0 copy-start.1
  17.5 0.0 copy-start.2
  17.5 32.7 %all_to_all.21 = bf16[16,224,256]{2,1,0:T(8,128)(2,1)S(1)} all-to-all(bf16[16,224,256]{2,1,0:T(8,128)(2,1)} %pack_arrived.1), channel_id=1, replica_groups=mesh['cluster'=8,'member'=16] {'member'}, dimensions={0} | all-to-all | bytes 3670016 | tf_op jit(solution)/shard_map/all_to_all | solution.py:557
  50.2 0.6 slice_reduce_fusion
  51.5 0.0 copy-done
  51.5 0.0 copy-done.1
  51.5 0.0 copy-done.2
  51.5 27.8 %conditional.1 = ((f32[144,2304]{1,0:T(8,128)}, f32[144]{0:T(256)})) conditional(s32[]{:T(128)} %convert_element_type.3, bf16[16,224,256]{2,1,0:T(8,128)(2,1)S(1)} %all_to_all.21, (bf16[144,512]{1,0:T(8,128)(2,1)S(1)}, bf16[48,512]{1,0:T(8,128)(2,1)S(1)}, bf16[16,512]{1,0:T(8,128)(2,1)S(1)}, bf16[16,512]{1,0:T(8,128)(2,1)S(1)}, ...), branch_computations={%region_1.0_spmd, %region_2.0_spmd} | conditional | flops 5505026 | bytes 22020188 | solution.py:562
  51.5 27.8 %system.2 = (f32[144,2304]{1,0:T(8,128)}, f32[144]{0:T(256)}) custom-call(s32[1]{0:T(128)} %bitcast.refs_0_, bf16[16,224,256]{2,1,0:T(8,128)(2,1)S(1)} %refs_1_), custom_call_target="tpu_custom_call" | custom-call | tf_op jit(solution)/shard_map/cond/branch_0_fun/system/pallas_call | solution.py:528
Async XLA Ops:
  2.8 11.0 %all-to-all-start.2 = ((bf16[8,16,256]{2,1,0:T(8,128)(2,1)}), bf16[8,16,256]{2,1,0:T(8,128)(2,1)S(1)}, u32[]{:S(2)}, u32[]{:S(2)}) async-start(bf16[8,16,256]{2,1,0:T(8,128)(2,1)} %bitcast.21), calls=%async_computation.2 | async-start | bytes 131072 | tf_op jit(solution)/shard_map/all_to_all | solution.py:471
  17.5 34.0 %copy-start = (bf16[18,8,512]{2,1,0:T(8,128)(2,1)S(1)}, bf16[18,8,512]{2,1,0:T(8,128)(2,1)}, u32[]{:S(2)}) copy-start(bf16[18,8,512]{2,1,0:T(8,128)(2,1)} %param.9) | copy-start | bytes 442372
  17.5 34.0 %copy-start.1 = (bf16[6,8,512]{2,1,0:T(8,128)(2,1)S(1)}, bf16[6,8,512]{2,1,0:T(8,128)(2,1)}, u32[]{:S(2)}) copy-start(bf16[6,8,512]{2,1,0:T(8,128)(2,1)} %param.10) | copy-start | bytes 147460
  17.5 34.0 %copy-start.2 = (bf16[2,8,512]{2,1,0:T(8,128)(2,1)S(1)}, bf16[2,8,512]{2,1,0:T(8,128)(2,1)}, u32[]{:S(2)}) copy-start(bf16[2,8,512]{2,1,0:T(8,128)(2,1)} %param.11) | copy-start | bytes 49156
